TPU v7x, 128 devices: a whole 4x4x4 slice. The times are simulated.
128 devices in a mesh: row: 8 (over y, core), col: 16 (over x, z).
Axes of the slice: x: 4, y: 4, z: 4, core: 2. Of those that a mesh axis runs over, the one named last changes fastest.
Arguments:
- visible_patches: bfloat16 [16, 256, 6144], P(None, 'row', 'col'), may hold values from -16 to 16
- input_gain: float32 [6144], P('col'), may hold values from 0.25 to 1.75
- encoder_project: bfloat16 [6144, 18432], P('col', 'row'), may hold values from -0.078125 to 0.078125
- query_gain: float32 [128], replicated, may hold values from 0.25 to 2.5
- key_gain: float32 [128], replicated, may hold values from 0.25 to 2.5
- output_weight: bfloat16 [6144, 6144], P('row', 'col'), may hold values from -0.30618622 to 0.30618622
- final_gain: float32 [6144], P('col'), may hold values from 0.25 to 2.5
- embed_weight: bfloat16 [6144, 1024], P('col'), may hold values from -0.078125 to 0.078125
- embed_bias: float32 [1024], replicated, may hold values from -3 to 3
- mask_token: float32 [1024], replicated, may hold values from -4 to 4
- position_embed: bfloat16 [1024, 1024], P('row'), may hold values from -3 to 3
- script_table: bfloat16 [40, 1024], replicated, may hold values from -3 to 3
- decoder_gain: float32 [1024], replicated, may hold values from 0.25 to 1.75
- decoder_project: bfloat16 [1024, 3072], replicated, may hold values from -0.1875 to 0.1875
- decoder_query: float32 [64], replicated, may hold values from 0.25 to 2.5
- decoder_key: float32 [64], replicated, may hold values from 0.25 to 2.5
- decoder_output: bfloat16 [1024, 1024], replicated, may hold values from -0.1875 to 0.1875
- head_gain: float32 [1024], replicated, may hold values from 0.25 to 1.75
- pixel_weight: bfloat16 [1024, 768], replicated, may hold values from -0.1875 to 0.1875
- pixel_bias: float32 [768], replicated, may hold values from -3 to 3
- visible_index: int32 [16, 256], P('col'), may hold values from 0 to 1023, as said below
- script_index: int32 [16], P('col'), may hold values from 0 to 39
Outputs:
- encoded: bfloat16 [16, 256, 6144], P(None, 'row', 'col')
- predicted: bfloat16 [16, 1024, 768], P('col', 'row')
Inputs may be any that keep to these rules, and one draw needn't show every extreme that they name: `visible_index`: each image's row holds 256 distinct patch positions in no particular order.
All inputs are finite; a program needn't handle non-finite values.
Results may differ from a plain program's by a relative error of at most 0.034.
Values may be sent and summed in bfloat16 or wider, within the bound.
A program may use at most 192 MiB of HBM per device.

v0:
```python
import jax
import jax.numpy as jnp
from jax import lax
from jax.sharding import PartitionSpec as P

D = 6144
DD = 1024


epsilon = 1e-06


def finish_norm(values, totals, squares, amount, gain_vector):
    average = totals / amount
    spread = squares / amount - average * average
    return (values - average) * lax.rsqrt(spread + epsilon) * gain_vector


def local_norm(values, gain_vector):
    average = jnp.mean(values, axis=-1, keepdims=True)
    spread = jnp.mean(values * values, axis=-1, keepdims=True) - average * average
    return (values - average) * lax.rsqrt(spread + epsilon) * gain_vector


def softmax_mix(queries, keys, values, factor):
    scores = (
        jnp.einsum("iqhd,ikhd->ihqk", queries, keys, preferred_element_type=jnp.float32) * factor
    )
    weights = jnp.exp(scores).astype(jnp.bfloat16)
    totals = jnp.sum(weights.astype(jnp.float32), axis=-1)
    mixture = jnp.einsum("ihqk,ikhd->iqhd", weights, values, preferred_element_type=jnp.float32)
    return (mixture / jnp.transpose(totals, (0, 2, 1))[..., None]).astype(jnp.bfloat16)


def encoder_heads(projected, query_gain, key_gain):
    images, extent, columns = projected.shape
    head_dim = query_gain.shape[0]
    head_count = columns // (3 * head_dim)
    pieces = projected.reshape(images, extent, head_count, 3, head_dim)
    queries = local_norm(pieces[:, :, :, 0], query_gain).astype(jnp.bfloat16)
    keys = local_norm(pieces[:, :, :, 1], key_gain).astype(jnp.bfloat16)
    values = pieces[:, :, :, 2].astype(jnp.bfloat16)
    mixed = softmax_mix(queries, keys, values, head_dim ** (-0.5))
    return mixed.reshape(images, extent, head_count * head_dim)


def local(
    visible_patches,
    input_gain,
    encoder_project,
    query_gain,
    key_gain,
    output_weight,
    final_gain,
    embed_weight,
    embed_bias,
    mask_token,
    position_embed,
    script_table,
    decoder_gain,
    decoder_project,
    decoder_query,
    decoder_key,
    decoder_output,
    head_gain,
    pixel_weight,
    pixel_bias,
    visible_index,
    script_index,
):
    own_images = script_index.shape[0]
    inputs = visible_patches.astype(jnp.float32)
    totals, squares = lax.psum(
        (jnp.sum(inputs, axis=-1, keepdims=True), jnp.sum(inputs * inputs, axis=-1, keepdims=True)),
        "col",
    )
    normed = finish_norm(inputs, totals, squares, D, input_gain).astype(jnp.bfloat16)
    gathered = lax.all_gather(normed, "row", axis=1, tiled=True)
    window = gathered
    projected = lax.psum_scatter(
        jnp.einsum(
            "itd,do->ito", window, encoder_project, preferred_element_type=jnp.float32
        ).astype(jnp.bfloat16),
        "col",
        scatter_dimension=0,
        tiled=True,
    ).astype(jnp.float32)
    heads_out = encoder_heads(projected, query_gain, key_gain)
    terms = jnp.einsum(
        "itd,de->ite",
        lax.all_gather(heads_out, "col", axis=0, tiled=True),
        output_weight,
        preferred_element_type=jnp.float32,
    )
    residual = inputs + lax.psum_scatter(
        terms.astype(jnp.bfloat16), "row", scatter_dimension=1, tiled=True
    ).astype(jnp.float32)
    encoded = residual.astype(jnp.bfloat16)
    totals_final, squares_final = lax.psum(
        (
            jnp.sum(residual, axis=-1, keepdims=True),
            jnp.sum(residual * residual, axis=-1, keepdims=True),
        ),
        "col",
    )
    enc_normed = finish_norm(residual, totals_final, squares_final, D, final_gain).astype(
        jnp.bfloat16
    )
    window = enc_normed
    embedded = (
        lax.psum_scatter(
            jnp.einsum(
                "itd,de->ite", window, embed_weight, preferred_element_type=jnp.float32
            ).astype(jnp.bfloat16),
            "col",
            scatter_dimension=0,
            tiled=True,
        ).astype(jnp.float32)
        + embed_bias
    ).astype(jnp.bfloat16)
    visible_rows = lax.all_gather(embedded, "row", axis=1, tiled=True)
    extent = position_embed.shape[0]
    places = lax.axis_index("row") * extent + jnp.arange(extent, dtype=jnp.int32)
    select = (visible_index[:, None, :] == places[None, :, None]).astype(jnp.bfloat16)
    present = jnp.sum(select.astype(jnp.float32), axis=2, keepdims=True)
    gathered_rows = jnp.einsum(
        "ipk,ikd->ipd", select, visible_rows, preferred_element_type=jnp.float32
    )
    script_ids = jnp.arange(script_table.shape[0], dtype=jnp.int32)
    labels = (script_index[:, None] == script_ids[None, :]).astype(jnp.bfloat16)
    scripted = jnp.dot(labels, script_table, preferred_element_type=jnp.float32)
    tokens = (
        gathered_rows
        + (1.0 - present) * mask_token
        + position_embed.astype(jnp.float32)
        + scripted[:, None, :]
    )
    dec_normed = local_norm(tokens, decoder_gain).astype(jnp.bfloat16)
    decoder_proj = jnp.einsum(
        "ipd,de->ipe", dec_normed, decoder_project, preferred_element_type=jnp.float32
    )
    head_dim = decoder_query.shape[0]
    head_count = DD // head_dim
    pieces = decoder_proj.reshape(own_images, extent, head_count, 3, head_dim)
    queries = local_norm(pieces[:, :, :, 0], decoder_query).astype(jnp.bfloat16)
    keys = local_norm(pieces[:, :, :, 1], decoder_key).astype(jnp.bfloat16)
    values = pieces[:, :, :, 2].astype(jnp.bfloat16)
    factor = head_dim ** (-0.5)
    packed = jnp.stack(
        [
            queries.reshape(own_images, extent, DD),
            keys.reshape(own_images, extent, DD),
            values.reshape(own_images, extent, DD),
        ],
        axis=1,
    )
    received = lax.all_to_all(packed, "row", split_axis=3, concat_axis=2, tiled=True)
    records = received.shape[0]
    positions = received.shape[2]
    group = received.shape[3] // head_dim
    parts = received.reshape(records, 3, positions, group, head_dim)
    result = softmax_mix(parts[:, 0], parts[:, 1], parts[:, 2], factor)
    result = result.reshape(records, positions, group * head_dim)
    dec_attended = lax.all_to_all(result, "row", split_axis=1, concat_axis=2, tiled=True)
    decoded = tokens + jnp.einsum(
        "ipd,de->ipe", dec_attended, decoder_output, preferred_element_type=jnp.float32
    )
    head_normed = local_norm(decoded, head_gain).astype(jnp.bfloat16)
    predicted = (
        jnp.einsum("ipd,de->ipe", head_normed, pixel_weight, preferred_element_type=jnp.float32)
        + pixel_bias
    ).astype(jnp.bfloat16)
    return (encoded, predicted)


def solution(mesh):
    return jax.shard_map(
        local,
        mesh=mesh,
        in_specs=(
            P(None, "row", "col"),
            P("col"),
            P("col", "row"),
            P(),
            P(),
            P("row", "col"),
            P("col"),
            P("col", None),
            P(),
            P(),
            P("row", None),
            P(),
            P(),
            P(),
            P(),
            P(),
            P(),
            P(),
            P(),
            P(),
            P("col", None),
            P("col"),
        ),
        out_specs=(P(None, "row", "col"), P("col", "row", None)),
        check_vma=False,
    )
```

profile of v0, /device:TPU:1, one launch (start us, length us, event | category | flops | bytes accessed | tf_op | source)
XLA Modules:
  0.0 580.3 jit_solution(17842627078822435845)
XLA Ops:
  7.2 0.0 copy-start
  7.2 0.0 all-gather.3.cloned.1.call-start
  7.2 1.3 convert_reduce_fusion.2
  8.6 62.4 %all-reduce.3 = (f32[16,32,1]{1,0,2:T(8,128)S(1)}, f32[16,32,1]{1,0,2:T(8,128)S(1)}) all-reduce(f32[16,32,1]{1,0,2:T(8,128)S(1)} %bitcast.170, f32[16,32,1]{1,0,2:T(8,128)S(1)} %bitcast.169), channel_id=1, replica_groups=mesh['row'=8,'col'=16] {'col'}, use_global_device_ids=true, to_apply=%region_3.0 | all-reduce | flops 1024 | bytes 8192 | tf_op jit(solution)/shard_map/psum | solution.py:73
  71.0 2.0 fusion.11
  72.9 0.0 all-gather.3.cloned.1.call-update
  73.0 0.0 reduce-scatter.10.cloned.1.call-start
  73.0 38.9 %all-gather.3.cloned.1.call-done = bf16[16,256,384]{2,1,0:T(8,128)(2,1)} async-done(((bf16[16,32,384]{2,1,0:T(8,128)(2,1)}), bf16[16,256,384]{2,1,0:T(8,128)(2,1)}) %all-gather.3.cloned.1.call-update) | async-done | bytes 3145744 | tf_op jit(solution)/shard_map/all_gather | solution.py:78
  111.9 15.6 %convolution_convert_fusion = bf16[16,256,2304]{2,1,0:T(8,128)(2,1)} fusion(bf16[16,256,384]{2,1,0:T(8,128)(2,1)} %all-gather.3.cloned.1.call-done, bf16[384,2304]{1,0:T(8,128)(2,1)} %param.24), kind=kOutput, calls=%fused_computation | convolution fusion | flops 7257194496 | bytes 23789568 | tf_op jit(solution)/shard_map/itd,do->ito/dot_general | solution.py:81
  127.5 0.0 reduce-scatter.10.cloned.1.call-update
  127.5 0.0 all-gather.5.cloned.1.call-start
  127.6 120.9 %reduce-scatter.10.cloned.1.call-done = bf16[1,256,2304]{2,1,0:T(8,128)(2,1)} async-done(((bf16[16,256,2304]{2,1,0:T(8,128)(2,1)}), bf16[1,256,2304]{2,1,0:T(8,128)(2,1)}) %reduce-scatter.10.cloned.1.call-update) | async-done | bytes 1179664
  248.4 1.6 copy.65
  250.0 0.0 copy-start.17
  250.0 0.3 reshape.615
  250.3 0.2 slice_reduce_fusion.1
  250.5 0.2 copy-done.16
  250.7 0.0 copy-done.17
  250.7 0.6 convert_reduce_fusion.1
  251.2 1.0 fusion.8
  252.3 1.9 copy.70
  254.2 0.0 all-gather.5.cloned.1.call-update
  254.3 0.0 reduce-scatter.8.cloned.1.call-start
  254.3 61.2 %all-gather.5.cloned.1.call-done = bf16[16,256,768]{2,1,0:T(8,128)(2,1)} async-done(((bf16[1,256,768]{2,1,0:T(8,128)(2,1)}), bf16[16,256,768]{2,1,0:T(8,128)(2,1)}) %all-gather.5.cloned.1.call-update) | async-done | bytes 6291472 | tf_op jit(solution)/shard_map/all_gather | solution.py:91
  315.5 8.0 %convolution_convert_fusion.1 = bf16[16,256,384]{2,1,0:T(8,128)(2,1)} fusion(bf16[16,256,768]{2,1,0:T(8,128)(2,1)} %all-gather.5.cloned.1.call-done, bf16[768,384]{1,0:T(8,128)(2,1)} %param.27), kind=kOutput, calls=%fused_computation.3 | convolution fusion | flops 2417491968 | bytes 10027008 | tf_op jit(solution)/shard_map/itd,de->ite/dot_general | solution.py:89
  323.5 0.0 reduce-scatter.8.cloned.1.call-update
  323.5 0.0 reduce-scatter.12.cloned.1.call-start
  323.6 32.5 %reduce-scatter.8.cloned.1.call-done = bf16[16,32,384]{2,1,0:T(8,128)(2,1)} async-done(((bf16[16,256,384]{2,1,0:T(8,128)(2,1)}), bf16[16,32,384]{2,1,0:T(8,128)(2,1)}) %reduce-scatter.8.cloned.1.call-update) | async-done | bytes 393232 | tf_op jit(solution)/shard_map/reduce_scatter | solution.py:95
  356.0 1.9 fusion.20
  358.0 60.7 %all-reduce.2 = (f32[16,32,1]{1,0,2:T(8,128)S(1)}, f32[16,32,1]{1,0,2:T(8,128)S(1)}) all-reduce(f32[16,32,1]{1,0,2:T(8,128)S(1)} %bitcast.168, f32[16,32,1]{1,0,2:T(8,128)S(1)} %bitcast.167), channel_id=1, replica_groups=mesh['row'=8,'col'=16] {'col'}, use_global_device_ids=true, to_apply=%region_14.0 | all-reduce | flops 1024 | bytes 8192 | tf_op jit(solution)/shard_map/psum | solution.py:99
  418.7 2.8 convolution_convert_fusion.2
  421.5 0.0 reduce-scatter.12.cloned.1.call-update
  422.1 0.0 copy-start.11
  422.2 0.0 copy-start.9
  422.2 8.7 %copy.71 = bf16[1024,3072]{0,1:T(8,128)(2,1)} copy(bf16[1024,3072]{1,0:T(8,128)(2,1)} %param.35) | data formatting | bytes 12582912 | tf_op args[13]
  431.0 0.1 mul.387
  431.0 0.1 mul.396
  431.1 0.2 convert_reduce_fusion.3
  431.3 0.1 fusion.46
  431.5 71.7 %reduce-scatter.12.cloned.1.call-done = bf16[1,32,1024]{2,1,0:T(8,128)(2,1)} async-done(((bf16[16,32,1024]{2,1,0:T(8,128)(2,1)}), bf16[1,32,1024]{2,1,0:T(8,128)(2,1)}) %reduce-scatter.12.cloned.1.call-update) | async-done | bytes 65552
  503.1 0.9 add_convert_fusion
  504.0 15.6 %all_gather.11 = bf16[1,256,1024]{2,1,0:T(8,128)(2,1)S(1)} all-gather(bf16[1,32,1024]{2,1,0:T(8,128)(2,1)S(1)} %add_convert_fusion), channel_id=1, replica_groups=mesh['row'=8,'col'=16] {'row'}, dimensions={1}, use_global_device_ids=true | all-gather | bytes 589824 | tf_op jit(solution)/shard_map/all_gather | solution.py:121
  519.6 0.4 fusion.52
  520.0 4.7 convolution_bitcast_fusion
  524.7 0.3 slice_reduce_fusion.3
  525.1 0.4 copy.74
  525.6 3.0 multiply_convert_fusion.3
  528.7 3.0 multiply_convert_fusion.2
  531.7 1.8 pad_maximum_fusion
  533.5 18.7 %all_to_all.30 = bf16[1,3,128,1024]{2,1,0,3:T(4,128)(2,1)S(1)} all-to-all(bf16[1,3,128,1024]{2,1,0,3:T(4,128)(2,1)S(1)} %pad_maximum_fusion), channel_id=1, replica_groups=mesh['row'=8,'col'=16] {'row'}, dimensions={3} | all-to-all | bytes 1572864 | tf_op jit(solution)/shard_map/all_to_all | solution.py:157
  552.2 0.6 copy.87
  552.9 1.2 reshape.618
  554.1 2.6 convert_reduce_fusion
  556.7 0.8 fusion.6
  557.6 0.4 copy.77
  558.0 0.5 broadcast.371
  558.5 2.2 reduce.29
  560.7 0.1 reshape.632
  560.8 9.9 %all_to_all.31 = bf16[8,2,8192]{2,1,0:T(2,128)(2,1)S(1)} all-to-all(bf16[8,2,8192]{2,1,0:T(2,128)(2,1)S(1)} %reshape.632), channel_id=1, replica_groups=mesh['row'=8,'col'=16] {'row'}, dimensions={0} | all-to-all | bytes 524288 | tf_op jit(solution)/shard_map/all_to_all | solution.py:164
  570.7 0.3 reshape.633
  571.1 0.2 copy.78
  571.3 0.6 fusion.51
  571.9 0.8 copy-done.2
  572.7 1.1 fusion.4
  (46 shorter events, 0.4 us)
Async XLA Ops:
  7.2 564.1 %copy-start = (bf16[1024,1024]{1,0:T(8,128)(2,1)S(1)}, bf16[1024,1024]{1,0:T(8,128)(2,1)}, u32[]{:S(2)}) copy-start(bf16[1024,1024]{1,0:T(8,128)(2,1)} %param.38) | copy-start | bytes 6291460
  7.2 104.7 %all-gather.3.cloned.1.call-start = ((), (), s32[]{:S(2)}) async-start(), calls=%async_computation.5 | async-start | bytes 3538944 | tf_op jit(solution)/shard_map/all_gather | solution.py:78
  73.0 175.5 %reduce-scatter.10.cloned.1.call-start = ((), (), s32[]{:S(2)}) async-start(), calls=%async_computation.8 | async-start | bytes 20054016
  127.5 188.0 %all-gather.5.cloned.1.call-start = ((), (), s32[]{:S(2)}) async-start(), calls=%async_computation.6 | async-start | bytes 6684672 | tf_op jit(solution)/shard_map/all_gather | solution.py:91
  250.0 0.7 copy-start.16
  250.0 0.7 copy-start.17
  254.3 101.8 %reduce-scatter.8.cloned.1.call-start = ((), (), s32[]{:S(2)}) async-start(), calls=%async_computation.7 | async-start | bytes 3538944 | tf_op jit(solution)/shard_map/reduce_scatter | solution.py:95
  323.5 32.5 %copy-start.1 = (bf16[16,32,384]{2,1,0:T(8,128)(2,1)S(1)}, bf16[16,32,384]{2,1,0:T(8,128)(2,1)}, u32[]{:S(2)}) copy-start(bf16[16,32,384]{2,1,0:T(8,128)(2,1)} %param.22) | copy-start | bytes 1179652
  323.5 95.2 %copy-start.12 = (bf16[384,1024]{1,0:T(8,128)(2,1)S(1)}, bf16[384,1024]{1,0:T(8,128)(2,1)}, u32[]{:S(2)}) copy-start(bf16[384,1024]{1,0:T(8,128)(2,1)} %param.29) | copy-start | bytes 2359300
  323.5 95.2 %copy-start.15 = (f32[384]{0:T(512)S(1)}, f32[384]{0:T(512)}, u32[]{:S(2)}) copy-start(f32[384]{0:T(512)} %param.28) | copy-start | bytes 4612
  323.5 179.6 %reduce-scatter.12.cloned.1.call-start = ((), (), s32[]{:S(2)}) async-start(), calls=%async_computation.9 | async-start | bytes 1114112
  422.1 8.8 %copy-start.10 = (f32[64]{0:T(128)S(1)}, f32[64]{0:T(128)}, u32[]{:S(2)}) copy-start(f32[64]{0:T(128)} %param.36) | copy-start | bytes 772
  422.1 8.9 %copy-start.11 = (f32[64]{0:T(128)S(1)}, f32[64]{0:T(128)}, u32[]{:S(2)}) copy-start(f32[64]{0:T(128)} %param.37) | copy-start | bytes 772
  422.2 9.0 %copy-start.9 = (s32[1,256]{1,0:T(1,128)S(1)}, s32[1,256]{1,0:T(1,128)}, u32[]{:S(2)}) copy-start(s32[1,256]{1,0:T(1,128)} %param.42) | copy-start | bytes 3076
  422.2 9.1 %copy-start.4 = (bf16[40,1024]{1,0:T(8,128)(2,1)S(1)}, bf16[40,1024]{1,0:T(8,128)(2,1)}, u32[]{:S(2)}) copy-start(bf16[40,1024]{1,0:T(8,128)(2,1)} %param.33) | copy-start | bytes 245764
  422.2 81.0 %copy-start.8 = (f32[1024]{0:T(1024)S(1)}, f32[1024]{0:T(1024)}, u32[]{:S(2)}) copy-start(f32[1024]{0:T(1024)} %param.30) | copy-start | bytes 12292
  422.2 97.4 %copy-start.13 = (bf16[128,1024]{1,0:T(8,128)(2,1)S(1)}, bf16[128,1024]{1,0:T(8,128)(2,1)}, u32[]{:S(2)}) copy-start(bf16[128,1024]{1,0:T(8,128)(2,1)} %param.32) | copy-start | bytes 786436
  422.2 97.4 %copy-start.14 = (f32[1024]{0:T(1024)S(1)}, f32[1024]{0:T(1024)}, u32[]{:S(2)}) copy-start(f32[1024]{0:T(1024)} %param.31) | copy-start | bytes 12292
  422.2 97.8 %copy-start.5 = (f32[1024]{0:T(1024)S(1)}, f32[1024]{0:T(1024)}, u32[]{:S(2)}) copy-start(f32[1024]{0:T(1024)} %param.34) | copy-start | bytes 12292
  554.1 2.7 copy-start.3
  571.0 0.9 copy-start.6
  571.0 0.8 copy-start.7
  571.3 1.4 copy-start.2
Sparse Core Ops, SparseCore 0:
  73.1 38.7 all-gather.2
  127.6 120.7 reduce-scatter.9
  254.4 61.0 all-gather.4
  323.6 32.3 reduce-scatter.7
  421.6 81.5 reduce-scatter.11
where the time goes:
time: 581 us; the launch traced here: 580 us
  waiting for transfers between devices  325 us (56%)
  blocking collectives  167 us (29%)
  matrix products  38.4 us (7%)
  local copies, waits for them, and re-layouts  17.3 us (3%)
  other arithmetic  17.1 us (3%)
  between operations  14.8 us (3%)
    unnamed x7, waiting for transfers between devices  193 us
    psum x1, blocking collectives, local(): lax.psum((jnp.sum(inputs, axis=-1, keepdims=True), jnp.sum(inputs * input...  62.4 us
    all_gather x1, waiting for transfers between devices, local(): lax.all_gather(heads_out, 'col', axis=0, tiled=True)  61.2 us
    psum x1, blocking collectives, local(): lax.psum((jnp.sum(residual, axis=-1, keepdims=True), jnp.sum(residual * r...  60.7 us
    all_gather x1, waiting for transfers between devices, local(): gathered = lax.all_gather(normed, 'row', axis=1, tiled=True)  38.9 us
    reduce_scatter x1, waiting for transfers between devices, local(): lax.psum_scatter(terms.astype(jnp.bfloat16), 'row', scatter_dimension=1,...  32.5 us
    all_to_all x1, blocking collectives, local(): lax.all_to_all(packed, 'row', split_axis=3, concat_axis=2, tiled=True)  18.7 us
    dot_general x1, matrix products, local(): jnp.einsum('itd,do->ito', window, encoder_project, preferred_element_type...  15.6 us
  transfers between devices with their start and end apart: 5, of which 5 were waited for; matrix products, arithmetic and copies ran while one was open for 2% of the time, Pallas kernels for 0%

commit v1 on v0

--- a/solution.py
+++ b/solution.py
@@ -1,13 +1,337 @@
+import functools
 import jax
 import jax.numpy as jnp
 from jax import lax
+from jax.experimental import pallas as pl
+from jax.experimental.pallas import tpu as pltpu
 from jax.sharding import PartitionSpec as P
 
 D = 6144
 DD = 1024
-
+MESH = pl.DeviceIdType.MESH
+bf16 = jnp.bfloat16
+f32 = jnp.float32
 
 epsilon = 1e-06
+LAST = (((1,), (1,)), ((), ()))
+
+
+def place():
+    row, col = lax.axis_index("row"), lax.axis_index("col")
+    return col // 4, row // 2, lax.rem(col, 4), lax.rem(row, 2)
+
+
+def turn(i, by):
+    return lax.rem(i + by, 4)
+
+
+def device(x, y, z, c):
+    return (y * 2 + c, x * 4 + z)
+
+
+def remote(src, dst, send_sem, recv_sem, where):
+    return pltpu.make_async_remote_copy(
+        src_ref=src,
+        dst_ref=dst,
+        send_sem=send_sem,
+        recv_sem=recv_sem,
+        device_id=where,
+        device_id_type=MESH,
+    )
+
+
+def greet(peers):
+    barrier = pltpu.get_barrier_semaphore()
+    for peer in peers:
+        pl.semaphore_signal(barrier, inc=1, device_id=peer, device_id_type=MESH)
+    return lambda: pl.semaphore_wait(barrier, len(peers))
+
+
+def aligned(index, multiple):
+    return pl.multiple_of(index, multiple)
+
+
+def row_sums(values):
+    ones = jnp.ones((8, values.shape[1]), bf16)
+    return lax.dot_general(ones, values, LAST, preferred_element_type=f32)
+
+
+def head_norm(values, gain_vector):
+    amount = values.shape[-1]
+    average = jnp.sum(values, axis=-1, keepdims=True) / amount
+    spread = jnp.sum(values * values, axis=-1, keepdims=True) / amount - average * average
+    return (values - average) * lax.rsqrt(spread + epsilon) * gain_vector
+
+
+def attention(queries, keys, values, factor):
+    scores = lax.dot_general(queries, keys, LAST, preferred_element_type=f32) * factor
+    weights = jnp.exp(scores).astype(bf16)
+    totals = jnp.sum(weights.astype(f32), axis=-1, keepdims=True)
+    mixture = jnp.dot(weights, values, preferred_element_type=f32)
+    return (mixture / totals).astype(bf16)
+
+
+HEADS_OWN = 6
+
+
+def encoder_kernel(
+    x_ref, gain_ref, w_ref, qg_ref, kg_ref, out_ref,
+    stats, normed, a, w, cs, cr,
+    w_own, st_s, st_r, ax_s, ax_r, ay_s, ay_r, ac_s, ac_r, wn_s, wn_r, wf_s, wf_r, c_s, c_r,
+):
+    x, y, z, c = place()
+    col = x * 4 + z
+    mate = device(x, y, z, 1 - c)
+    right, left = turn(x, 1), turn(x, 3)
+
+    def col_peer(d):
+        other = lax.rem(col + d, 16)
+        return device(other // 4, y, lax.rem(other, 4), c)
+
+    entered = greet(
+        [col_peer(d) for d in range(1, 16)]
+        + [device(x, turn(y, e), z, c) for e in range(1, 4)]
+        + [mate]
+    )
+
+    def w_block(j, owner, start, size):
+        return w.at[j, pl.ds(aligned(owner * 384 + start, 192), size), :]
+
+    def w_fetch(j):
+        return pltpu.make_async_copy(
+            w_ref.at[:, pl.ds(aligned(j * 384, 128), 384)], w_block(j, x, 0, 384), w_own.at[j]
+        )
+
+    def w_send(j, way):
+        block = w_block(j, x, 0, 384)
+        target = device(right if way == 0 else left, y, z, c)
+        return remote(block, block, wn_s.at[way, j], wn_r.at[way, j], target)
+
+    def w_got(j, way):
+        block = w_block(j, left if way == 0 else right, 0, 384)
+        return remote(block, block, wn_s.at[way, j], wn_r.at[way, j], mate)
+
+    def w_forward(j, way):
+        block = w_block(j, left if way == 0 else right, 192 * way, 192)
+        target = device(right if way == 0 else left, y, z, c)
+        return remote(block, block, wf_s.at[way, j], wf_r.at[way, j], target)
+
+    def w_far(j, way):
+        block = w_block(j, turn(x, 2), 192 * way, 192)
+        return remote(block, block, wf_s.at[way, j], wf_r.at[way, j], mate)
+
+    def w_start(j):
+        w_fetch(j).wait()
+        w_send(j, 0).start()
+        w_send(j, 1).start()
+
+    def w_step(j):
+        w_got(j, 0).wait_recv()
+        w_forward(j, 0).start()
+        w_got(j, 1).wait_recv()
+        w_forward(j, 1).start()
+
+        @pl.when(j + 2 < HEADS_OWN)
+        def _():
+            w_start(j + 2)
+
+    @pl.loop(0, HEADS_OWN)
+    def _(j):
+        w_fetch(j).start()
+
+    values = x_ref[...].reshape(512, 384)
+    wide = values.astype(f32)
+    square = wide * wide
+    high = square.astype(bf16)
+    low = (square - high.astype(f32)).astype(bf16)
+    sums = row_sums(values)
+    squares = row_sums(high) + row_sums(low)
+    stats[col] = jnp.concatenate(
+        [sums[0:1, i * 128 : i * 128 + 128] for i in range(4)]
+        + [squares[0:1, i * 128 : i * 128 + 128] for i in range(4)],
+        axis=0,
+    )
+
+    entered()
+
+    def stat_copy(d, owner):
+        block = stats.at[owner]
+        return remote(block, block, st_s.at[d], st_r.at[d], col_peer(d))
+
+    @pl.loop(1, 16)
+    def _(d):
+        stat_copy(d, col).start()
+
+    w_start(0)
+    w_start(1)
+
+    @pl.loop(1, 16)
+    def _(d):
+        stat_copy(d, lax.rem(col + 16 - d, 16)).wait_recv()
+
+    totals = jnp.sum(stats[...], axis=0) / D
+    average = totals[0:4]
+    rate = lax.rsqrt(totals[4:8] - average * average + epsilon)
+    turned = jnp.transpose(jnp.concatenate([average, rate], axis=0))
+    for g in range(4):
+        block = x_ref[4 * g : 4 * g + 4].reshape(128, 384).astype(f32)
+        block = (block - turned[:, g : g + 1]) * turned[:, g + 4 : g + 5] * gain_ref[...]
+        normed[g] = block.astype(bf16)
+
+    def a_block(owner):
+        return a.at[y, c, :, pl.ds(aligned(owner * 384, 128), 384)]
+
+    def ax_copy(d):
+        return remote(
+            normed.at[turn(x, d)], a_block(x), ax_s.at[d], ax_r.at[d], device(turn(x, d), y, z, c)
+        )
+
+    def ax_got(d):
+        block = a_block(turn(x, 4 - d))
+        return remote(block, block, ax_s.at[d], ax_r.at[d], mate)
+
+    for d in (1, 3, 2):
+        ax_copy(d).start()
+    a[y, c, :, pl.ds(aligned(x * 384, 128), 384)] = normed[x]
+
+    def spread_rows(owner):
+        block = a_block(owner)
+        for e in (1, 3, 2):
+            remote(block, block, ay_s.at[e], ay_r.at[e], device(x, turn(y, e), z, c)).start()
+        remote(block, block, ac_s.at[0], ac_r.at[0], mate).start()
+
+    spread_rows(x)
+    w_step(0)
+    for d in (1, 3, 2):
+        ax_got(d).wait_recv()
+        spread_rows(turn(x, 4 - d))
+    w_step(1)
+
+    def c_copy(j, s, d):
+        rows = pl.ds(aligned(s * 64, 64), 64)
+        owner = turn(z, d)
+        return remote(
+            cs.at[j, owner, rows, :],
+            cr.at[d - 1, j, rows, :],
+            c_s.at[d - 1, j],
+            c_r.at[d - 1, j],
+            device(x, y, owner, c),
+        )
+
+    def c_all(j, d):
+        return remote(
+            cs.at[j, turn(z, d)], cr.at[d - 1, j], c_s.at[d - 1, j], c_r.at[d - 1, j], mate
+        )
+
+    def attend_head(j):
+        for d in range(1, 4):
+            c_all(j, d).wait_recv()
+        projected = cs[j, z].astype(f32)
+        for d in range(3):
+            projected = projected + cr[d, j].astype(f32)
+        queries = head_norm(projected[:, 0:128], qg_ref[...]).astype(bf16)
+        keys = head_norm(projected[:, 128:256], kg_ref[...]).astype(bf16)
+        out_ref[j] = attention(queries, keys, projected[:, 256:384].astype(bf16), 128 ** (-0.5))
+
+    @pl.loop(0, HEADS_OWN)
+    def _(j):
+        w_far(j, 0).wait_recv()
+        w_far(j, 1).wait_recv()
+
+        @pl.loop(0, 4)
+        def _(i):
+            e = i + (i // 2) * (5 - 2 * i)
+            s = turn(y, 4 - e)
+
+            @pl.when(j == 0)
+            def _():
+                @pl.when(i > 0)
+                def _():
+                    got = a.at[s, c]
+                    remote(got, got, ay_s.at[e], ay_r.at[e], mate).wait_recv()
+                    remote(got, got, ac_s.at[e], ac_r.at[e], mate).start()
+
+                other = a.at[s, 1 - c]
+                remote(other, other, ac_s.at[e], ac_r.at[e], mate).wait_recv()
+
+            product = jnp.dot(a[s].reshape(256, 1536), w[j], preferred_element_type=f32).astype(bf16)
+            for core in range(2):
+                for image in range(4):
+                    first = core * 128 + image * 32
+                    rows = pl.ds(aligned(s * 64 + core * 32, 32), 32)
+                    cs[j, image, rows, :] = product[first : first + 32]
+            for d in (1, 3, 2):
+                c_copy(j, s, d).start()
+
+        @pl.when(j + 2 < HEADS_OWN)
+        def _():
+            w_step(j + 2)
+
+        @pl.when(j > 0)
+        def _():
+            attend_head(j - 1)
+
+    attend_head(HEADS_OWN - 1)
+
+    @pl.loop(1, 16)
+    def _(d):
+        stat_copy(d, col).wait_send()
+
+    for d in range(1, 4):
+        ax_copy(d).wait_send()
+    for e in range(4):
+        whole = a.at[turn(y, 4 - e), c]
+        if e > 0:
+            remote(whole, whole, ay_s.at[e], ay_r.at[e], mate).wait_send()
+        remote(whole, whole, ac_s.at[e], ac_r.at[e], mate).wait_send()
+
+    @pl.loop(0, HEADS_OWN)
+    def _(j):
+        for way in range(2):
+            w_send(j, way).wait_send()
+            w_forward(j, way).wait_send()
+        for d in range(1, 4):
+            c_all(j, d).wait_send()
+
+
+VMEM = pl.BlockSpec(memory_space=pltpu.VMEM)
+ANY = pl.BlockSpec(memory_space=pl.ANY)
+DMA = pltpu.SemaphoreType.DMA
+
+
+def encoder_heads(visible_patches, input_gain, encoder_project, query_gain, key_gain):
+    return pl.pallas_call(
+        encoder_kernel,
+        out_shape=jax.ShapeDtypeStruct((HEADS_OWN, 256, 128), bf16),
+        in_specs=[VMEM, VMEM, ANY, VMEM, VMEM],
+        out_specs=VMEM,
+        scratch_shapes=[
+            pltpu.VMEM((16, 8, 128), f32),
+            pltpu.VMEM((4, 128, 384), bf16),
+            pltpu.VMEM((4, 2, 128, 1536), bf16),
+            pltpu.VMEM((HEADS_OWN, 1536, 384), bf16),
+            pltpu.VMEM((HEADS_OWN, 4, 256, 384), bf16),
+            pltpu.VMEM((3, HEADS_OWN, 256, 384), bf16),
+            DMA((HEADS_OWN,)),
+            DMA((16,)), DMA((16,)),
+            DMA((4,)), DMA((4,)),
+            DMA((4,)), DMA((4,)),
+            DMA((4,)), DMA((4,)),
+            DMA((2, HEADS_OWN)), DMA((2, HEADS_OWN)),
+            DMA((2, HEADS_OWN)), DMA((2, HEADS_OWN)),
+            DMA((3, HEADS_OWN)), DMA((3, HEADS_OWN)),
+        ],
+        compiler_params=pltpu.CompilerParams(
+            collective_id=0, has_side_effects=True, vmem_limit_bytes=56 << 20
+        ),
+        name="encoder_heads",
+    )(
+        visible_patches,
+        input_gain.reshape(1, 384),
+        encoder_project,
+        query_gain.reshape(1, 128),
+        key_gain.reshape(1, 128),
+    )
 
 
 def finish_norm(values, totals, squares, amount, gain_vector):
@@ -30,18 +354,6 @@
     totals = jnp.sum(weights.astype(jnp.float32), axis=-1)
     mixture = jnp.einsum("ihqk,ikhd->iqhd", weights, values, preferred_element_type=jnp.float32)
     return (mixture / jnp.transpose(totals, (0, 2, 1))[..., None]).astype(jnp.bfloat16)
-
-
-def encoder_heads(projected, query_gain, key_gain):
-    images, extent, columns = projected.shape
-    head_dim = query_gain.shape[0]
-    head_count = columns // (3 * head_dim)
-    pieces = projected.reshape(images, extent, head_count, 3, head_dim)
-    queries = local_norm(pieces[:, :, :, 0], query_gain).astype(jnp.bfloat16)
-    keys = local_norm(pieces[:, :, :, 1], key_gain).astype(jnp.bfloat16)
-    values = pieces[:, :, :, 2].astype(jnp.bfloat16)
-    mixed = softmax_mix(queries, keys, values, head_dim ** (-0.5))
-    return mixed.reshape(images, extent, head_count * head_dim)
 
 
 def local(
@@ -70,22 +382,8 @@
 ):
     own_images = script_index.shape[0]
     inputs = visible_patches.astype(jnp.float32)
-    totals, squares = lax.psum(
-        (jnp.sum(inputs, axis=-1, keepdims=True), jnp.sum(inputs * inputs, axis=-1, keepdims=True)),
-        "col",
-    )
-    normed = finish_norm(inputs, totals, squares, D, input_gain).astype(jnp.bfloat16)
-    gathered = lax.all_gather(normed, "row", axis=1, tiled=True)
-    window = gathered
-    projected = lax.psum_scatter(
-        jnp.einsum(
-            "itd,do->ito", window, encoder_project, preferred_element_type=jnp.float32
-        ).astype(jnp.bfloat16),
-        "col",
-        scatter_dimension=0,
-        tiled=True,
-    ).astype(jnp.float32)
-    heads_out = encoder_heads(projected, query_gain, key_gain)
+    heads_out = encoder_heads(visible_patches, input_gain, encoder_project, query_gain, key_gain)
+    heads_out = jnp.transpose(heads_out, (1, 0, 2)).reshape(1, 256, 768)
     terms = jnp.einsum(
         "itd,de->ite",
         lax.all_gather(heads_out, "col", axis=0, tiled=True),

time: 581 us -> 430 us (0.74)
  waiting for transfers between devices: 325 us -> 162 us
  Pallas kernels: 0 us -> 95.1 us
  blocking collectives: 167 us -> 105 us
  matrix products: 38.4 us -> 22.5 us
    unnamed x7 -> x4, waiting for transfers between devices: 193 us -> 71.8 us
    pallas_call x0 -> x1, Pallas kernels: none -> 95.1 us  [encoder_heads(): pl.pallas_call(encoder_kernel, out_shape=jax.ShapeDtypeStruct((HEADS_OWN,...]
    psum x1 -> x0, blocking collectives: 62.4 us -> none  [local(): lax.psum((jnp.sum(inputs, axis=-1, keepdims=True), jnp.sum(inputs * input...]
    all_gather x1 -> x0, waiting for transfers between devices: 38.9 us -> none  [local(): gathered = lax.all_gather(normed, 'row', axis=1, tiled=True)]
    dot_general x1 -> x0, matrix products: 15.6 us -> none  [local(): jnp.einsum('itd,do->ito', window, encoder_project, preferred_element_type...]
  transfers between devices with their start and end apart: 5 -> 3, of which waited for: 5 -> 3; matrix products, arithmetic and copies ran while one was open for 2% -> 2% of each run, Pallas kernels for 0% -> 0%
where the time goes in v1:
time: 430 us; the launch traced here: 429 us
  waiting for transfers between devices  162 us (38%)
  blocking collectives  105 us (24%)
  Pallas kernels  95.1 us (22%)
  matrix products  22.5 us (5%)
  local copies, waits for them, and re-layouts  16.4 us (4%)
  between operations  14.8 us (3%)
  other arithmetic  13.3 us (3%)
    pallas_call x1, Pallas kernels, encoder_heads(): pl.pallas_call(encoder_kernel, out_shape=jax.ShapeDtypeStruct((HEADS_OWN,...  95.1 us
    unnamed x4, waiting for transfers between devices  71.8 us
    psum x1, blocking collectives, local(): lax.psum((jnp.sum(residual, axis=-1, keepdims=True), jnp.sum(residual * r...  60.7 us
    all_gather x1, waiting for transfers between devices, local(): lax.all_gather(heads_out, 'col', axis=0, tiled=True)  57.4 us
    reduce_scatter x1, waiting for transfers between devices, local(): lax.psum_scatter(terms.astype(jnp.bfloat16), 'row', scatter_dimension=1,...  32.5 us
    all_to_all x1, blocking collectives, local(): lax.all_to_all(packed, 'row', split_axis=3, concat_axis=2, tiled=True)  18.7 us
    all_gather x1, blocking collectives, local(): visible_rows = lax.all_gather(embedded, 'row', axis=1, tiled=True)  15.7 us
    all_to_all x1, blocking collectives, local(): lax.all_to_all(result, 'row', split_axis=1, concat_axis=2, tiled=True)  9.94 us
  transfers between devices with their start and end apart: 3, of which 3 were waited for; matrix products, arithmetic and copies ran while one was open for 2% of the time, Pallas kernels for 0%

profile of v1, /device:TPU:1, one launch (start us, length us, event | category | flops | bytes accessed | tf_op | source)
XLA Modules:
  0.0 428.9 jit_solution(3208502434764594414)
XLA Ops:
  7.2 0.0 copy-start
  7.2 0.0 copy-start.12
  7.2 0.0 all-gather.2.cloned.1.call-start
  7.2 1.4 reshape.492.gain_ref
  8.7 95.1 %encoder_heads.1 = bf16[6,256,128]{2,1,0:T(8,128)(2,1)} custom-call(bf16[16,32,384]{2,1,0:T(8,128)(2,1)} %x_ref.1, f32[1,384]{1,0:T(1,128)} %reshape.492.gain_ref, bf16[384,2304]{1,0:T(8,128)(2,1)} %w_ref.1, f32[1,128]{1,0:T(1,128)} %bitcast.122, f32[1,128]{1,0:T(1,128)} %bitcast.123), custom_call_target="tpu_custom_call" | custom-call | tf_op jit(solution)/shard_map/encoder_heads/pallas_call | solution.py:303
  103.8 1.2 copy.49
  105.0 0.9 copy.50
  105.9 0.0 all-gather.2.cloned.1.call-update
  105.9 0.0 copy-start.1
  105.9 0.0 reduce-scatter.5.cloned.1.call-start
  106.0 57.4 %all-gather.2.cloned.1.call-done = bf16[16,256,768]{2,1,0:T(8,128)(2,1)} async-done(((bf16[1,256,768]{2,1,0:T(8,128)(2,1)}), bf16[16,256,768]{2,1,0:T(8,128)(2,1)}) %all-gather.2.cloned.1.call-update) | async-done | bytes 6291472 | tf_op jit(solution)/shard_map/all_gather | solution.py:389
  163.4 0.0 copy-done.12
  163.4 7.9 %convolution_convert_fusion = bf16[16,256,384]{2,1,0:T(8,128)(2,1)} fusion(bf16[16,256,768]{2,1,0:T(8,128)(2,1)} %all-gather.2.cloned.1.call-done, bf16[768,384]{1,0:T(8,128)(2,1)S(1)} %copy-done.12), kind=kOutput, calls=%fused_computation.2 | convolution fusion | flops 2417491968 | bytes 10027008 | tf_op jit(solution)/shard_map/itd,de->ite/dot_general | solution.py:387
  171.3 0.0 reduce-scatter.5.cloned.1.call-update
  171.3 0.0 reduce-scatter.7.cloned.1.call-start
  171.4 32.5 %reduce-scatter.5.cloned.1.call-done = bf16[16,32,384]{2,1,0:T(8,128)(2,1)} async-done(((bf16[16,256,384]{2,1,0:T(8,128)(2,1)}), bf16[16,32,384]{2,1,0:T(8,128)(2,1)}) %reduce-scatter.5.cloned.1.call-update) | async-done | bytes 393232 | tf_op jit(solution)/shard_map/reduce_scatter | solution.py:393
  203.8 0.0 copy-done.1
  203.8 1.9 fusion.7
  205.8 60.7 %all-reduce.1 = (f32[16,32,1]{1,0,2:T(8,128)S(1)}, f32[16,32,1]{1,0,2:T(8,128)S(1)}) all-reduce(f32[16,32,1]{1,0,2:T(8,128)S(1)} %bitcast.118, f32[16,32,1]{1,0,2:T(8,128)S(1)} %bitcast.117), channel_id=1, replica_groups=mesh['row'=8,'col'=16] {'col'}, use_global_device_ids=true, to_apply=%region_4.0 | all-reduce | flops 1024 | bytes 8192 | tf_op jit(solution)/shard_map/psum | solution.py:397
  266.5 0.0 copy-done.11
  266.5 0.0 copy-done.15
  266.5 2.8 convolution_convert_fusion.1
  269.3 0.0 reduce-scatter.7.cloned.1.call-update
  269.9 0.0 copy-start.9
  269.9 0.0 copy-start.10
  270.0 0.0 copy-start.8
  270.0 0.0 copy-start.3
  270.0 0.0 copy-start.7
  270.0 0.0 copy-start.13
  270.0 0.0 copy-start.14
  270.0 0.0 copy-start.4
  270.0 8.7 %copy.51 = bf16[1024,3072]{0,1:T(8,128)(2,1)} copy(bf16[1024,3072]{1,0:T(8,128)(2,1)} %param.35) | data formatting | bytes 12582912 | tf_op args[13]
  278.8 0.0 copy-done.9
  278.8 0.1 mul.251
  278.8 0.1 mul.260
  278.9 0.2 convert_reduce_fusion.1
  279.1 0.1 fusion.25
  279.3 71.8 %reduce-scatter.7.cloned.1.call-done = bf16[1,32,1024]{2,1,0:T(8,128)(2,1)} async-done(((bf16[16,32,1024]{2,1,0:T(8,128)(2,1)}), bf16[1,32,1024]{2,1,0:T(8,128)(2,1)}) %reduce-scatter.7.cloned.1.call-update) | async-done | bytes 65552
  351.0 0.9 add_convert_fusion
  351.9 15.7 %all_gather.7 = bf16[1,256,1024]{2,1,0:T(8,128)(2,1)S(1)} all-gather(bf16[1,32,1024]{2,1,0:T(8,128)(2,1)S(1)} %add_convert_fusion), channel_id=1, replica_groups=mesh['row'=8,'col'=16] {'row'}, dimensions={1}, use_global_device_ids=true | all-gather | bytes 589824 | tf_op jit(solution)/shard_map/all_gather | solution.py:419
  367.6 0.0 copy-done.13
  367.6 0.4 fusion.31
  368.0 4.7 %convolution_bitcast_fusion = f32[1,128,16,3,64]{1,4,3,2,0:T(8,128)S(1)} fusion(bf16[16,3,64,1024]{3,2,1,0:T(8,128)(2,1)} %bitcast.100, f32[128,1024]{1,0:T(8,128)S(1)} %get-tuple-element.27, f32[1024]{0:T(1024)S(1)} %copy-done.4, f32[128]{0:T(128)S(1)} %get-tuple-element.26, f32[128]{0:T(128)S(1)} %get-tuple-element.25), kind=kOutput, calls=%fused_computation.3 | convolution fusion | flops 805830656 | bytes 8393728 | tf_op jit(solution)/shard_map/ipd,de->ipe/dot_general | solution.py:437
  372.8 0.3 slice_reduce_fusion.1
  373.1 0.4 copy.54
  373.6 3.0 multiply_convert_fusion.3
  376.7 3.0 multiply_convert_fusion.2
  379.7 1.8 pad_maximum_fusion
  381.5 18.7 %all_to_all.30 = bf16[1,3,128,1024]{2,1,0,3:T(4,128)(2,1)S(1)} all-to-all(bf16[1,3,128,1024]{2,1,0,3:T(4,128)(2,1)S(1)} %pad_maximum_fusion), channel_id=1, replica_groups=mesh['row'=8,'col'=16] {'row'}, dimensions={3} | all-to-all | bytes 1572864 | tf_op jit(solution)/shard_map/all_to_all | solution.py:455
  400.2 0.6 copy.63
  400.9 1.2 reshape.497
  402.1 2.6 convert_reduce_fusion
  404.7 0.8 fusion.5
  405.6 0.0 copy-start.5
  405.6 0.0 copy-start.6
  405.6 0.4 copy.57
  406.0 0.5 broadcast.274
  406.5 2.2 reduce.19
  408.8 0.1 reshape.509
  408.8 9.9 %all_to_all.31 = bf16[8,2,8192]{2,1,0:T(2,128)(2,1)S(1)} all-to-all(bf16[8,2,8192]{2,1,0:T(2,128)(2,1)S(1)} %reshape.509), channel_id=1, replica_groups=mesh['row'=8,'col'=16] {'row'}, dimensions={0} | all-to-all | bytes 524288 | tf_op jit(solution)/shard_map/all_to_all | solution.py:462
  418.8 0.3 reshape.510
  419.1 0.2 copy.58
  419.3 0.6 fusion.30
  419.9 2.5 fusion.3
  (27 shorter events, 0.3 us)
Async XLA Ops:
  7.2 412.1 %copy-start = (bf16[1024,1024]{1,0:T(8,128)(2,1)S(1)}, bf16[1024,1024]{1,0:T(8,128)(2,1)}, u32[]{:S(2)}) copy-start(bf16[1024,1024]{1,0:T(8,128)(2,1)} %param.38) | copy-start | bytes 6291460
  7.2 156.2 %copy-start.12 = (bf16[768,384]{1,0:T(8,128)(2,1)S(1)}, bf16[768,384]{1,0:T(8,128)(2,1)}, u32[]{:S(2)}) copy-start(bf16[768,384]{1,0:T(8,128)(2,1)} %param.27) | copy-start | bytes 1769476
  7.2 156.2 %all-gather.2.cloned.1.call-start = ((), (), s32[]{:S(2)}) async-start(), calls=%async_computation.4 | async-start | bytes 6684672 | tf_op jit(solution)/shard_map/all_gather | solution.py:389
  105.9 97.9 %copy-start.1 = (bf16[16,32,384]{2,1,0:T(8,128)(2,1)S(1)}, bf16[16,32,384]{2,1,0:T(8,128)(2,1)}, u32[]{:S(2)}) copy-start(bf16[16,32,384]{2,1,0:T(8,128)(2,1)} %x_ref.1) | copy-start | bytes 1179652
  105.9 97.9 %reduce-scatter.5.cloned.1.call-start = ((), (), s32[]{:S(2)}) async-start(), calls=%async_computation.5 | async-start | bytes 3538944 | tf_op jit(solution)/shard_map/reduce_scatter | solution.py:393
  171.3 95.2 %copy-start.11 = (bf16[384,1024]{1,0:T(8,128)(2,1)S(1)}, bf16[384,1024]{1,0:T(8,128)(2,1)}, u32[]{:S(2)}) copy-start(bf16[384,1024]{1,0:T(8,128)(2,1)} %param.29) | copy-start | bytes 2359300
  171.3 95.2 %copy-start.15 = (f32[384]{0:T(512)S(1)}, f32[384]{0:T(512)}, u32[]{:S(2)}) copy-start(f32[384]{0:T(512)} %param.28) | copy-start | bytes 4612
  171.3 179.7 %reduce-scatter.7.cloned.1.call-start = ((), (), s32[]{:S(2)}) async-start(), calls=%async_computation.6 | async-start | bytes 1114112
  269.9 8.8 %copy-start.9 = (f32[64]{0:T(128)S(1)}, f32[64]{0:T(128)}, u32[]{:S(2)}) copy-start(f32[64]{0:T(128)} %param.36) | copy-start | bytes 772
  269.9 8.9 %copy-start.10 = (f32[64]{0:T(128)S(1)}, f32[64]{0:T(128)}, u32[]{:S(2)}) copy-start(f32[64]{0:T(128)} %param.37) | copy-start | bytes 772
  270.0 9.0 %copy-start.8 = (s32[1,256]{1,0:T(1,128)S(1)}, s32[1,256]{1,0:T(1,128)}, u32[]{:S(2)}) copy-start(s32[1,256]{1,0:T(1,128)} %param.42) | copy-start | bytes 3076
  270.0 9.1 %copy-start.3 = (bf16[40,1024]{1,0:T(8,128)(2,1)S(1)}, bf16[40,1024]{1,0:T(8,128)(2,1)}, u32[]{:S(2)}) copy-start(bf16[40,1024]{1,0:T(8,128)(2,1)} %param.33) | copy-start | bytes 245764
  270.0 81.0 %copy-start.7 = (f32[1024]{0:T(1024)S(1)}, f32[1024]{0:T(1024)}, u32[]{:S(2)}) copy-start(f32[1024]{0:T(1024)} %param.30) | copy-start | bytes 12292
  270.0 97.6 %copy-start.13 = (bf16[128,1024]{1,0:T(8,128)(2,1)S(1)}, bf16[128,1024]{1,0:T(8,128)(2,1)}, u32[]{:S(2)}) copy-start(bf16[128,1024]{1,0:T(8,128)(2,1)} %param.32) | copy-start | bytes 786436
  270.0 97.6 %copy-start.14 = (f32[1024]{0:T(1024)S(1)}, f32[1024]{0:T(1024)}, u32[]{:S(2)}) copy-start(f32[1024]{0:T(1024)} %param.31) | copy-start | bytes 12292
  270.0 98.0 %copy-start.4 = (f32[1024]{0:T(1024)S(1)}, f32[1024]{0:T(1024)}, u32[]{:S(2)}) copy-start(f32[1024]{0:T(1024)} %param.34) | copy-start | bytes 12292
  402.1 2.7 copy-start.2
  405.6 14.3 %copy-start.5 = (f32[1024]{0:T(1024)S(1)}, f32[1024]{0:T(1024)}, u32[]{:S(2)}) copy-start(f32[1024]{0:T(1024)} %param.39) | copy-start | bytes 12292
  405.6 14.3 %copy-start.6 = (f32[768]{0:T(1024)S(1)}, f32[768]{0:T(1024)}, u32[]{:S(2)}) copy-start(f32[768]{0:T(1024)} %param.41) | copy-start | bytes 9220
Sparse Core Ops, SparseCore 0:
  106.0 57.2 all-gather.1
  171.4 32.3 reduce-scatter.4
  269.4 81.5 reduce-scatter.6

commit v2 on v1

v2 whole, which is shorter than its diff:
```python
import jax
import jax.numpy as jnp
from jax import lax
from jax.experimental import pallas as pl
from jax.experimental.pallas import tpu as pltpu
from jax.sharding import PartitionSpec as P

D = 6144
DD = 1024
HEADS_OWN = 6
CHUNKS = 8
MESH = pl.DeviceIdType.MESH
bf16 = jnp.bfloat16
f32 = jnp.float32

epsilon = 1e-06
LAST = (((1,), (1,)), ((), ()))


def turn(i, by):
    return lax.rem(i + by, 4)


def near(i):
    return i + (i // 2) * (5 - 2 * i)


def device(x, y, z, c):
    return (y * 2 + c, x * 4 + z)


def remote(src, dst, send_sem, recv_sem, where):
    return pltpu.make_async_remote_copy(
        src_ref=src,
        dst_ref=dst,
        send_sem=send_sem,
        recv_sem=recv_sem,
        device_id=where,
        device_id_type=MESH,
    )


def aligned(index, multiple):
    return pl.multiple_of(index, multiple)


def norm(values, gain_vector):
    amount = values.shape[-1]
    average = jnp.sum(values, axis=-1, keepdims=True) / amount
    spread = jnp.sum(values * values, axis=-1, keepdims=True) / amount - average * average
    return (values - average) * lax.rsqrt(spread + epsilon) * gain_vector


def pair_norm(values, gain_vector):
    first = lax.broadcasted_iota(jnp.int32, values.shape, 1) < 64

    def mean(v):
        one = jnp.sum(jnp.where(first, v, 0.0), axis=-1, keepdims=True)
        two = jnp.sum(jnp.where(first, 0.0, v), axis=-1, keepdims=True)
        return jnp.where(first, one, two) / 64

    average = mean(values)
    spread = mean(values * values) - average * average
    return (values - average) * lax.rsqrt(spread + epsilon) * gain_vector


def attention(queries, keys, values, factor):
    scores = lax.dot_general(queries, keys, LAST, preferred_element_type=f32) * factor
    weights = jnp.exp(scores).astype(bf16)
    totals = jnp.sum(weights.astype(f32), axis=-1, keepdims=True)
    mixture = jnp.dot(weights, values, preferred_element_type=f32)
    return (mixture / totals).astype(bf16)


def kernel(
    x_ref, ig_ref, w_ref, qg_ref, kg_ref, wo_ref, fg_ref, ew_ref, eb_ref, mask_ref, pos_ref,
    script_ref, dg_ref, dp_ref, dqg_ref, dkg_ref, do_ref, hg_ref, pw_ref, pb_ref, vi_ref, si_ref,
    enc_ref, pred_ref,
    gains, raw, stats, a, w, cs, cr, att, po, pr, yr, res, en, es, ew, pos, dpw, dow, pxw,
    eo, er, vis, tok, dq, dk, dv, dm, da,
    l_s, w_s, g_s, g_r, x_s, x_r, st_s, st_r, ay_s, ay_r, ac_s, ac_r, wn_s, wn_r, wf_s, wf_r,
    c_s, c_r, t_s, t_r, p_s, p_r, pc_s, pc_r, ex_s, ex_r, ey_s, ey_r, ec_s, ec_r,
    m_s, m_r, y_s, y_r, en_s, en_r, eb_s, eb_r, v_s, v_r, d_s, d_r,
):
    row, col = lax.axis_index("row"), lax.axis_index("col")
    x, y, z, c = col // 4, row // 2, lax.rem(col, 4), lax.rem(row, 2)
    mate = device(x, y, z, 1 - c)
    right, left = turn(x, 1), turn(x, 3)

    def x_peer(d):
        return device(turn(x, d), y, z, c)

    def y_peer(d):
        return device(x, turn(y, d), z, c)

    def z_peer(d):
        return device(x, y, turn(z, d), c)

    def row_peer(e, m):
        return device(x, turn(y, e), z, c + m - 2 * c * m)

    def row_from(e, m):
        return turn(y, 4 - e) * 2 + c + m - 2 * c * m

    def w_block(j, owner, start, size):
        return w.at[j, pl.ds(aligned(owner * 384 + start, 192), size), :]

    def w_fetch(j):
        return pltpu.make_async_copy(
            w_ref.at[:, pl.ds(aligned(j * 384, 128), 384)], w_block(j, x, 0, 384), w_s.at[j]
        )

    @pl.loop(0, HEADS_OWN)
    def _(j):
        w_fetch(j).start()

    fetches = [
        pltpu.make_async_copy(wo_ref.at[0:384], w_block(6, x, 0, 384), l_s.at[0]),
        pltpu.make_async_copy(wo_ref.at[384:768], w_block(7, x, 0, 384), l_s.at[1]),
        pltpu.make_async_copy(ew_ref, ew.at[x], l_s.at[2]),
        pltpu.make_async_copy(pos_ref, pos.at[y, c], l_s.at[3]),
        pltpu.make_async_copy(
            dp_ref.at[:, pl.ds(aligned(row * 384, 128), 384)], dpw, l_s.at[4]
        ),
        pltpu.make_async_copy(do_ref, dow, l_s.at[5]),
        pltpu.make_async_copy(pw_ref, pxw, l_s.at[6]),
    ]
    for fetch in fetches:
        fetch.start()

    first_row = lax.broadcasted_iota(jnp.int32, (8, 384), 0) == 0
    gains[x] = jnp.where(first_row, ig_ref[...], fg_ref[...])
    raw[x] = x_ref[pl.ds(x * 4, 4)]

    barrier = pltpu.get_barrier_semaphore()
    peers = (
        [x_peer(d) for d in range(1, 4)]
        + [z_peer(d) for d in range(1, 4)]
        + [row_peer(k // 2, k % 2) for k in range(1, 8)]
    )
    for peer in peers:
        pl.semaphore_signal(barrier, inc=1, device_id=peer, device_id_type=MESH)
    pl.semaphore_wait(barrier, len(peers))

    def raw_copy(d):
        there = turn(x, d)
        return remote(x_ref.at[pl.ds(there * 4, 4)], raw.at[x], x_s.at[d], x_r.at[d], x_peer(d))

    def gain_copy(d):
        return remote(gains.at[x], gains.at[x], g_s.at[d], g_r.at[d], x_peer(d))

    for d in (1, 3, 2):
        gain_copy(d).start()
        raw_copy(d).start()

    def w_send(j, way):
        block = w_block(j, x, 0, 384)
        target = device(right if way == 0 else left, y, z, c)
        return remote(block, block, wn_s.at[way, j], wn_r.at[way, j], target)

    def w_got(j, way):
        block = w_block(j, left if way == 0 else right, 0, 384)
        return remote(block, block, wn_s.at[way, j], wn_r.at[way, j], mate)

    def w_forward(j, way):
        block = w_block(j, left if way == 0 else right, 192 * way, 192)
        target = device(right if way == 0 else left, y, z, c)
        return remote(block, block, wf_s.at[way, j], wf_r.at[way, j], target)

    def w_far(j, way):
        block = w_block(j, turn(x, 2), 192 * way, 192)
        return remote(block, block, wf_s.at[way, j], wf_r.at[way, j], mate)

    def w_start(j):
        w_send(j, 0).start()
        w_send(j, 1).start()

    def w_step(j):
        w_got(j, 0).wait_recv()
        w_forward(j, 0).start()
        w_got(j, 1).wait_recv()
        w_forward(j, 1).start()

        @pl.when(j + 2 < CHUNKS)
        def _():
            w_start(j + 2)

    @pl.loop(0, HEADS_OWN)
    def _(j):
        w_fetch(j).wait()

    fetches[0].wait()
    fetches[1].wait()
    w_start(0)
    w_start(1)

    def stat_copy(n, d, owner):
        block = stats.at[n, owner]
        return remote(block, block, st_s.at[n, d], st_r.at[n, d], z_peer(d))

    def share_stats(n, total, square):
        lane = lax.broadcasted_iota(jnp.int32, (128, 128), 1)
        stats[n, z] = jnp.transpose(jnp.where(lane == 0, total, square))[0:8]
        for d in (1, 3, 2):
            stat_copy(n, d, z).start()
        for d in (1, 3, 2):
            stat_copy(n, d, turn(z, 4 - d)).wait_recv()
        sums = jnp.transpose(jnp.sum(stats[n], axis=0))
        average = sums[:, 0:1] / D
        spread = sums[:, 1:2] / D - average * average
        return average, lax.rsqrt(spread + epsilon)

    for d in (1, 3, 2):
        there = turn(x, 4 - d)
        remote(gains.at[there], gains.at[there], g_s.at[d], g_r.at[d], mate).wait_recv()
        remote(raw.at[there], raw.at[there], x_s.at[d], x_r.at[d], mate).wait_recv()
    total, square = 0.0, 0.0
    for g in range(4):
        block = raw[g].reshape(128, 384).astype(f32)
        total = total + jnp.sum(block, axis=-1, keepdims=True)
        square = square + jnp.sum(block * block, axis=-1, keepdims=True)
    average, rate = share_stats(0, total, square)
    for g in range(4):
        block = raw[g].reshape(128, 384).astype(f32)
        block = (block - average) * rate * gains[g, 0:1, :]
        a[y, c, :, 384 * g : 384 * g + 384] = block.astype(bf16)

    def spread_rows(block, s_y, r_y, s_c, r_c):
        for e in (1, 3, 2):
            remote(block, block, s_y.at[e], r_y.at[e], y_peer(e)).start()
        remote(block, block, s_c.at[0], r_c.at[0], mate).start()

    spread_rows(a.at[y, c], ay_s, ay_r, ac_s, ac_r)
    w_step(0)
    w_step(1)

    def c_copy(j, s, d):
        rows = pl.ds(aligned(s * 64, 64), 64)
        return remote(
            cs.at[j, turn(z, d), rows, :],
            cr.at[d - 1, j, rows, :],
            c_s.at[d - 1, j],
            c_r.at[d - 1, j],
            z_peer(d),
        )

    def c_all(j, d):
        return remote(
            cs.at[j, turn(z, d)], cr.at[d - 1, j], c_s.at[d - 1, j], c_r.at[d - 1, j], mate
        )

    def t_copy(j, d):
        block = att.at[z, :, pl.ds(aligned(j * 128, 128), 128)]
        return remote(block, block, t_s.at[d], t_r.at[d], z_peer(d))

    def attend_head(j):
        for d in range(1, 4):
            c_all(j, d).wait_recv()
        projected = cs[j, z].astype(f32)
        for d in range(3):
            projected = projected + cr[d, j].astype(f32)
        queries = norm(projected[:, 0:128], qg_ref[...]).astype(bf16)
        keys = norm(projected[:, 128:256], kg_ref[...]).astype(bf16)
        mixed = attention(queries, keys, projected[:, 256:384].astype(bf16), 128 ** (-0.5))
        att[z, :, pl.ds(aligned(j * 128, 128), 128)] = mixed
        for d in (1, 3, 2):
            t_copy(j, d).start()

    def ew_part(owner, part):
        return ew.at[owner, pl.ds(aligned(part * 48, 16), 48), :]

    def ex_copy(d):
        block = ew_part(x, row)
        return remote(block, block, ex_s.at[d], ex_r.at[d], x_peer(d))

    def ex_got(d):
        block = ew_part(turn(x, 4 - d), row)
        return remote(block, block, ex_s.at[d], ex_r.at[d], mate)

    def ey_copy(d, e):
        block = ew_part(turn(x, 4 - d), row)
        return remote(block, block, ey_s.at[d, e], ey_r.at[d, e], y_peer(e))

    def ey_got(d, e):
        block = ew_part(turn(x, 4 - d), turn(y, 4 - e) * 2 + c)
        return remote(block, block, ey_s.at[d, e], ey_r.at[d, e], mate)

    def ec_copy(d, e):
        block = ew_part(turn(x, 4 - d), turn(y, 4 - e) * 2 + c)
        return remote(block, block, ec_s.at[d, e], ec_r.at[d, e], mate)

    def ec_got(d, e):
        block = ew_part(turn(x, 4 - d), turn(y, 4 - e) * 2 + 1 - c)
        return remote(block, block, ec_s.at[d, e], ec_r.at[d, e], mate)

    @pl.loop(0, HEADS_OWN)
    def _(j):
        w_far(j, 0).wait_recv()
        w_far(j, 1).wait_recv()

        @pl.loop(0, 4)
        def _(i):
            e = near(i)
            s = turn(y, 4 - e)

            @pl.when(j == 0)
            def _():
                @pl.when(i > 0)
                def _():
                    got = a.at[s, c]
                    remote(got, got, ay_s.at[e], ay_r.at[e], mate).wait_recv()
                    remote(got, got, ac_s.at[e], ac_r.at[e], mate).start()

                other = a.at[s, 1 - c]
                remote(other, other, ac_s.at[e], ac_r.at[e], mate).wait_recv()

            product = jnp.dot(a[s].reshape(256, 1536), w[j], preferred_element_type=f32).astype(bf16)
            for core in range(2):
                for image in range(4):
                    first = core * 128 + image * 32
                    rows = pl.ds(aligned(s * 64 + core * 32, 32), 32)
                    cs[j, image, rows, :] = product[first : first + 32]
            for d in (1, 3, 2):
                c_copy(j, s, d).start()

        @pl.when(j == 1)
        def _():
            fetches[2].wait()
            fetches[3].wait()
            spread_rows(pos.at[y, c], p_s, p_r, pc_s, pc_r)
            for d in (1, 3, 2):
                ex_copy(d).start()

        @pl.when(j == 3)
        def _():
            for e in (1, 3, 2):
                got = pos.at[turn(y, 4 - e), c]
                remote(got, got, p_s.at[e], p_r.at[e], mate).wait_recv()
                remote(got, got, pc_s.at[e], pc_r.at[e], mate).start()
            for d in (1, 3, 2):
                ex_got(d).wait_recv()
                for e in (1, 3, 2):
                    ey_copy(d, e).start()
                ec_copy(d, 0).start()

        @pl.when(j > 0)
        def _():
            attend_head(j - 1)

        w_step(j + 2)

    attend_head(HEADS_OWN - 1)
    for e in (1, 3, 2):
        for d in (1, 3, 2):
            ey_got(d, e).wait_recv()
            ec_copy(d, e).start()
    for d in (1, 3, 2):
        whole = att.at[turn(z, 4 - d)]
        remote(whole, whole, t_s.at[d], t_r.at[d], mate).wait_recv()

    def block_at(i):
        return turn(x, 4 - near(i))

    def mate_copy(i):
        there = block_at(i)
        return remote(po.at[there, 1 - c], pr.at[there], m_s.at[i], m_r.at[i], mate)

    def y_copy(i, e):
        there = block_at(i)
        return remote(
            po.at[there, c, turn(y, e)], yr.at[e - 1, there], y_s.at[e, i], y_r.at[e, i], y_peer(e)
        )

    def reduce_rows(i):
        there = block_at(i)
        mate_copy(i).wait_recv()
        both = po[there, c].astype(f32) + pr[there].astype(f32)
        po[there, c] = both.astype(bf16)
        for e in (1, 3, 2):
            y_copy(i, e).start()

    @pl.loop(0, 4)
    def _(i):
        there = block_at(i)

        @pl.when(i == 3)
        def _():
            for j in (6, 7):
                w_far(j, 0).wait_recv()
                w_far(j, 1).wait_recv()

        rows = pl.ds(aligned(there * 384, 384), 384)
        both = att[...].reshape(1024, 768)
        product = jnp.dot(both[:, 0:384], w[6, rows, :], preferred_element_type=f32)
        product = product + jnp.dot(both[:, 384:768], w[7, rows, :], preferred_element_type=f32)
        product = product.astype(bf16)
        for image in range(4):
            for part in range(8):
                first = image * 256 + part * 32
                po[there, part % 2, part // 2, image * 32 : image * 32 + 32, :] = product[
                    first : first + 32
                ]
        mate_copy(i).start()

        @pl.when(i > 0)
        def _():
            reduce_rows(i - 1)

    reduce_rows(3)

    res[...] = jnp.zeros_like(res)

    def enc_copy(d):
        there = turn(x, d)
        return remote(
            es.at[there], enc_ref.at[pl.ds(x * 4, 4)], en_s.at[d], en_r.at[d], x_peer(d)
        )

    total, square = 0.0, 0.0
    for i in range(4):
        there = block_at(i)
        for e in (1, 3, 2):
            y_copy(i, e).wait_recv()
        block = raw[there].reshape(128, 384).astype(f32) + po[there, c, y].astype(f32)
        for e in range(3):
            block = block + yr[e, there].astype(f32)
        res[there] = block
        es[there] = block.astype(bf16).reshape(4, 32, 384)
        total = total + jnp.sum(block, axis=-1, keepdims=True)
        square = square + jnp.sum(block * block, axis=-1, keepdims=True)
    average, rate = share_stats(1, total, square)
    for g in range(4):
        block = (res[g] - average) * rate * gains[g, 1:2, :]
        en[:, 384 * g : 384 * g + 384] = block.astype(bf16)
    for d in (1, 3, 2):
        enc_copy(d).start()
    enc_ref[pl.ds(x * 4, 4)] = es[x]

    for d in (1, 3, 2):
        for e in range(4):
            ec_got(d, e).wait_recv()
    product = jnp.dot(en[...], ew[...].reshape(1536, DD), preferred_element_type=f32)
    eo[...] = product.astype(bf16).reshape(4, 32, DD)

    def eb_copy(d):
        return remote(eo.at[turn(z, d)], er.at[d - 1], eb_s.at[d], eb_r.at[d], z_peer(d))

    for d in (1, 3, 2):
        eb_copy(d).start()
    embedded = eo[z].astype(f32)
    for d in (1, 3, 2):
        eb_copy(d).wait_recv()
        embedded = embedded + er[d - 1].astype(f32)
    vis[row] = (embedded + eb_ref[...]).astype(bf16)

    def vis_copy(k):
        block = vis.at[row]
        return remote(block, block, v_s.at[k], v_r.at[k], row_peer(k // 2, k % 2))

    for k in (4, 5, 2, 3, 6, 7, 1):
        vis_copy(k).start()

    ids = lax.broadcasted_iota(jnp.int32, script_ref.shape, 0)
    scripted = jnp.sum(
        jnp.where(ids == si_ref[...], script_ref[...].astype(f32), 0.0), axis=0, keepdims=True
    )
    fetches[4].wait()
    for e in range(4):
        got = pos.at[turn(y, 4 - e), 1 - c]
        remote(got, got, pc_s.at[e], pc_r.at[e], mate).wait_recv()
    dv[:, 128:256] = jnp.ones((1024, 128), bf16)
    for k in range(1, 8):
        block = vis.at[row_from(k // 2, k % 2)]
        remote(block, block, v_s.at[k], v_r.at[k], mate).wait_recv()
    query_gain = jnp.concatenate([dqg_ref[...], dqg_ref[...]], axis=1)
    key_gain = jnp.concatenate([dkg_ref[...], dkg_ref[...]], axis=1)

    @pl.loop(0, 4)
    def _(i):
        rows = pl.ds(aligned(i * 256, 256), 256)
        positions = lax.broadcasted_iota(jnp.int32, (256, 256), 0) + i * 256
        select = jnp.where(positions == vi_ref[...], 1.0, 0.0)
        present = jnp.sum(select, axis=1, keepdims=True)
        tokens = jnp.dot(
            select.astype(bf16), vis[...].reshape(256, DD), preferred_element_type=f32
        )
        tokens = tokens + (1.0 - present) * mask_ref[...]
        tokens = tokens + pos[i].reshape(256, DD).astype(f32) + scripted
        tok[rows, :] = tokens
        normed = norm(tokens, dg_ref[...]).astype(bf16)
        made = jnp.dot(normed, dpw[...], preferred_element_type=f32)
        queries = jnp.concatenate([made[:, 0:64], made[:, 192:256]], axis=1)
        keys = jnp.concatenate([made[:, 64:128], made[:, 256:320]], axis=1)
        values = jnp.concatenate([made[:, 128:192], made[:, 320:384]], axis=1)
        queries = pair_norm(queries, query_gain)
        first = lax.broadcasted_iota(jnp.int32, queries.shape, 1) < 64
        dq[0, rows, :] = jnp.where(first, queries, 0.0).astype(bf16)
        dq[1, rows, :] = jnp.where(first, 0.0, queries).astype(bf16)
        dk[rows, :] = pair_norm(keys, key_gain).astype(bf16)
        dv[rows, 0:128] = values.astype(bf16)

    def mix_copy(e, m):
        owner = turn(y, e) * 2 + c + m - 2 * c * m
        block = da.at[:, pl.ds(aligned(row * 128, 128), 128)]
        return remote(dm.at[owner], block, d_s.at[e, m], d_r.at[e, m], row_peer(e, m))

    def mix_got(e, m):
        block = da.at[:, pl.ds(aligned(row_from(e, m) * 128, 128), 128)]
        return remote(block, block, d_s.at[e, m], d_r.at[e, m], mate)

    @pl.loop(0, 4)
    def _(i):
        e = near(3 - i)
        there = turn(y, e)
        rows = pl.ds(aligned(there * 256, 256), 256)
        mixtures = []
        for h in range(2):
            scores = lax.dot_general(dq[h, rows, :], dk[...], LAST, preferred_element_type=f32)
            weights = jnp.exp(scores * 64 ** (-0.5)).astype(bf16)
            both = jnp.dot(weights, dv[...], preferred_element_type=f32)
            mixtures.append(both[:, 0:128] / both[:, 128:256])
        first = lax.broadcasted_iota(jnp.int32, (256, 128), 1) < 64
        mixed = jnp.where(first, mixtures[0], mixtures[1]).astype(bf16)
        dm[there * 2] = mixed[0:128]
        dm[there * 2 + 1] = mixed[128:256]

        @pl.when(e > 0)
        def _():
            mix_copy(e, 0).start()

        mix_copy(e, 1).start()

    da[:, pl.ds(aligned(row * 128, 128), 128)] = dm[row]
    fetches[5].wait()
    fetches[6].wait()
    for k in range(1, 8):
        mix_got(k // 2, k % 2).wait_recv()
    decoded = tok[pl.ds(aligned(row * 128, 128), 128), :] + jnp.dot(
        da[...], dow[...], preferred_element_type=f32
    )
    normed = norm(decoded, hg_ref[...]).astype(bf16)
    predicted = jnp.dot(normed, pxw[...], preferred_element_type=f32) + pb_ref[...]
    pred_ref[0] = predicted.astype(bf16)

    for d in range(1, 4):
        block = enc_ref.at[pl.ds(turn(x, 4 - d) * 4, 4)]
        remote(block, block, en_s.at[d], en_r.at[d], mate).wait_recv()
        enc_copy(d).wait_send()
        gain_copy(d).wait_send()
        raw_copy(d).wait_send()
        stat_copy(0, d, z).wait_send()
        stat_copy(1, d, z).wait_send()
        ex_copy(d).wait_send()
        eb_copy(d).wait_send()
        whole = att.at[z]
        remote(whole, whole, t_s.at[d], t_r.at[d], mate).wait_send()
        ec_copy(d, 0).wait_send()
        for e in range(1, 4):
            ey_copy(d, e).wait_send()
            ec_copy(d, e).wait_send()
    for e in range(4):
        for block, s_y, r_y, s_c, r_c in (
            (a, ay_s, ay_r, ac_s, ac_r),
            (pos, p_s, p_r, pc_s, pc_r),
        ):
            if e > 0:
                own = block.at[y, c]
                remote(own, own, s_y.at[e], r_y.at[e], mate).wait_send()
            passed = block.at[turn(y, 4 - e), c]
            remote(passed, passed, s_c.at[e], r_c.at[e], mate).wait_send()
        mate_copy(e).wait_send()
        for i in range(1, 4):
            y_copy(e, i).wait_send()
    for k in range(1, 8):
        vis_copy(k).wait_send()
        mix_copy(k // 2, k % 2).wait_send()

    @pl.loop(0, CHUNKS)
    def _(j):
        for way in range(2):
            w_send(j, way).wait_send()
            w_forward(j, way).wait_send()

    @pl.loop(0, HEADS_OWN)
    def _(j):
        for d in range(1, 4):
            c_all(j, d).wait_send()


VMEM = pl.BlockSpec(memory_space=pltpu.VMEM)
ANY = pl.BlockSpec(memory_space=pl.ANY)


def local(
    visible_patches,
    input_gain,
    encoder_project,
    query_gain,
    key_gain,
    output_weight,
    final_gain,
    embed_weight,
    embed_bias,
    mask_token,
    position_embed,
    script_table,
    decoder_gain,
    decoder_project,
    decoder_query,
    decoder_key,
    decoder_output,
    head_gain,
    pixel_weight,
    pixel_bias,
    visible_index,
    script_index,
):
    def flat(vector):
        return vector.reshape(1, -1)

    dma = pltpu.SemaphoreType.DMA
    two = [dma((4,)), dma((4,))]
    return pl.pallas_call(
        kernel,
        out_shape=(
            jax.ShapeDtypeStruct((16, 32, 384), bf16),
            jax.ShapeDtypeStruct((1, 128, 768), bf16),
        ),
        in_specs=[
            VMEM, VMEM, ANY, VMEM, VMEM, ANY, VMEM, ANY, VMEM, VMEM, ANY,
            VMEM, VMEM, ANY, VMEM, VMEM, ANY, VMEM, ANY, VMEM, VMEM, VMEM,
        ],
        out_specs=(VMEM, VMEM),
        scratch_shapes=[
            pltpu.VMEM((4, 8, 384), f32),
            pltpu.VMEM((4, 4, 32, 384), bf16),
            pltpu.VMEM((2, 4, 8, 128), f32),
            pltpu.VMEM((4, 2, 128, 1536), bf16),
            pltpu.VMEM((CHUNKS, 1536, 384), bf16),
            pltpu.VMEM((HEADS_OWN, 4, 256, 384), bf16),
            pltpu.VMEM((3, HEADS_OWN, 256, 384), bf16),
            pltpu.VMEM((4, 256, 768), bf16),
            pltpu.VMEM((4, 2, 4, 128, 384), bf16),
            pltpu.VMEM((4, 4, 128, 384), bf16),
            pltpu.VMEM((3, 4, 128, 384), bf16),
            pltpu.VMEM((4, 128, 384), f32),
            pltpu.VMEM((128, 1536), bf16),
            pltpu.VMEM((4, 4, 32, 384), bf16),
            pltpu.VMEM((4, 384, DD), bf16),
            pltpu.VMEM((4, 2, 128, DD), bf16),
            pltpu.VMEM((DD, 384), bf16),
            pltpu.VMEM((DD, DD), bf16),
            pltpu.VMEM((DD, 768), bf16),
            pltpu.VMEM((4, 32, DD), bf16),
            pltpu.VMEM((3, 32, DD), bf16),
            pltpu.VMEM((8, 32, DD), bf16),
            pltpu.VMEM((1024, DD), f32),
            pltpu.VMEM((2, 1024, 128), bf16),
            pltpu.VMEM((1024, 128), bf16),
            pltpu.VMEM((1024, 256), bf16),
            pltpu.VMEM((8, 128, 128), bf16),
            pltpu.VMEM((128, DD), bf16),
            dma((7,)),
            dma((HEADS_OWN,)),
            *two,
            *two,
            dma((2, 4)), dma((2, 4)),
            *two,
            *two,
            dma((2, CHUNKS)), dma((2, CHUNKS)),
            dma((2, CHUNKS)), dma((2, CHUNKS)),
            dma((3, HEADS_OWN)), dma((3, HEADS_OWN)),
            *two,
            *two,
            *two,
            *two,
            dma((4, 4)), dma((4, 4)),
            dma((4, 4)), dma((4, 4)),
            *two,
            dma((4, 4)), dma((4, 4)),
            *two,
            *two,
            dma((8,)), dma((8,)),
            dma((4, 2)), dma((4, 2)),
        ],
        compiler_params=pltpu.CompilerParams(
            collective_id=0, has_side_effects=True, vmem_limit_bytes=62 << 20
        ),
        name="masked_patches",
    )(
        visible_patches, flat(input_gain), encoder_project, flat(query_gain), flat(key_gain),
        output_weight, flat(final_gain), embed_weight, flat(embed_bias), flat(mask_token),
        position_embed, script_table, flat(decoder_gain), decoder_project, flat(decoder_query),
        flat(decoder_key), decoder_output, flat(head_gain), pixel_weight, flat(pixel_bias),
        visible_index, flat(script_index),
    )


def solution(mesh):
    return jax.shard_map(
        local,
        mesh=mesh,
        in_specs=(
            P(None, "row", "col"),
            P("col"),
            P("col", "row"),
            P(),
            P(),
            P("row", "col"),
            P("col"),
            P("col", None),
            P(),
            P(),
            P("row", None),
            P(),
            P(),
            P(),
            P(),
            P(),
            P(),
            P(),
            P(),
            P(),
            P("col", None),
            P("col"),
        ),
        out_specs=(P(None, "row", "col"), P("col", "row", None)),
        check_vma=False,
    )
```

time: 430 us -> 171 us (0.40)
  waiting for transfers between devices: 162 us -> 0 us
  blocking collectives: 105 us -> 0 us
  Pallas kernels: 95.1 us -> 163 us
  matrix products: 22.5 us -> 0 us
  between operations: 14.8 us -> 1.29 us
  other arithmetic: 13.3 us -> 0 us
  local copies, waits for them, and re-layouts: 16.4 us -> 7.17 us
    unnamed x4 -> x0, waiting for transfers between devices: 71.8 us -> none
    pallas_call x1, Pallas kernels: 95.1 us -> 163 us  [local(): pl.pallas_call(kernel, out_shape=(jax.ShapeDtypeStruct((16, 32, 384), bf1...]
    psum x1 -> x0, blocking collectives: 60.7 us -> none  [local(): lax.psum((jnp.sum(residual, axis=-1, keepdims=True), jnp.sum(residual * r...]
    all_gather x1 -> x0, waiting for transfers between devices: 57.4 us -> none  [local(): lax.all_gather(heads_out, 'col', axis=0, tiled=True)]
    reduce_scatter x1 -> x0, waiting for transfers between devices: 32.5 us -> none  [local(): lax.psum_scatter(terms.astype(jnp.bfloat16), 'row', scatter_dimension=1,...]
    all_to_all x2 -> x0, blocking collectives: 28.6 us -> none  [the longest x1 18.7 us: local(): lax.all_to_all(packed, 'row', split_axis=3, concat_axis=2, tiled=True)]
    dot_general x9 -> x0, matrix products: 22.5 us -> none  [the longest x1 7.92 us: local(): jnp.einsum('itd,de->ite', lax.all_gather(heads_out, 'col', axis=0, tiled=...]
    all_gather x1 -> x0, blocking collectives: 15.7 us -> none  [local(): visible_rows = lax.all_gather(embedded, 'row', axis=1, tiled=True)]
  transfers between devices with their start and end apart: 3 -> 0, of which waited for: 3 -> 0; matrix products, arithmetic and copies ran while one was open for 2% -> 0% of each run, Pallas kernels for 0% -> 0%
where the time goes in v2:
time: 171 us
  Pallas kernels  163 us (95%)
  local copies, waits for them, and re-layouts  7.17 us (4%)
    pallas_call x1, Pallas kernels, local(): pl.pallas_call(kernel, out_shape=(jax.ShapeDtypeStruct((16, 32, 384), bf1...  163 us
    reshape x3, local copies, waits for them, and re-layouts, flat(): return vector.reshape(1, -1)  3.77 us

profile of v2, /device:TPU:1, one launch (start us, length us, event | category | flops | bytes accessed | tf_op | source)
XLA Modules:
  0.0 171.1 jit_solution(14617394992678941504)
XLA Ops:
  1.3 1.2 reshape.40.ig_ref
  2.5 1.3 reshape.43.fg_ref
  3.8 1.3 reshape.50.pb_ref
  5.0 162.7 %masked_patches.1 = (bf16[16,32,384]{2,1,0:T(8,128)(2,1)}, bf16[1,128,768]{2,1,0:T(8,128)(2,1)}) custom-call(bf16[16,32,384]{2,1,0:T(8,128)(2,1)} %x_ref.1, f32[1,384]{1,0:T(1,128)} %reshape.40.ig_ref, bf16[384,2304]{1,0:T(8,128)(2,1)} %w_ref.1, f32[1,128]{1,0:T(1,128)} %bitcast.14, f32[1,128]{1,0:T(1,128)} %bitcast.15, bf16[768,384]{1,0:T(8,128)(2,1)} %wo_ref.1, ...), custom_call_target="tpu_custom_call" | custom-call | tf_op jit(solution)/shard_map/masked_patches/pallas_call | solution.py:623
  167.7 1.8 %copy.27 = bf16[16,32,384]{2,1,0:T(8,128)(2,1)} copy(bf16[16,32,384]{2,1,0:T(8,128)(2,1)} %get-tuple-element.4) | data formatting | bytes 786432
  169.5 1.6 copy.28

commit v3 on v2

--- a/solution.py
+++ b/solution.py
@@ -76,10 +76,10 @@
     x_ref, ig_ref, w_ref, qg_ref, kg_ref, wo_ref, fg_ref, ew_ref, eb_ref, mask_ref, pos_ref,
     script_ref, dg_ref, dp_ref, dqg_ref, dkg_ref, do_ref, hg_ref, pw_ref, pb_ref, vi_ref, si_ref,
     enc_ref, pred_ref,
-    gains, raw, stats, a, w, cs, cr, att, po, pr, yr, res, en, es, ew, pos, dpw, dow, pxw,
-    eo, er, vis, tok, dq, dk, dv, dm, da,
+    gains, raw, stats, a, w, cs, cr, hop, att, po, pr, yr, res, en, es, ew, pos, dpw, dow, pxw,
+    eo, er, vis, scr, sel, tok, tokv, dq, dk, dv, base, vq, vk, vv, dm, da,
     l_s, w_s, g_s, g_r, x_s, x_r, st_s, st_r, ay_s, ay_r, ac_s, ac_r, wn_s, wn_r, wf_s, wf_r,
-    c_s, c_r, t_s, t_r, p_s, p_r, pc_s, pc_r, ex_s, ex_r, ey_s, ey_r, ec_s, ec_r,
+    h_s, h_r, c_s, c_r, t_s, t_r, p_s, p_r, pc_s, pc_r, ex_s, ex_r, ec_s, ec_r,
     m_s, m_r, y_s, y_r, en_s, en_r, eb_s, eb_r, v_s, v_r, d_s, d_r,
 ):
     row, col = lax.axis_index("row"), lax.axis_index("col")
@@ -231,34 +231,64 @@
         remote(block, block, s_c.at[0], r_c.at[0], mate).start()
 
     spread_rows(a.at[y, c], ay_s, ay_r, ac_s, ac_r)
+    fetches[3].wait()
+    spread_rows(pos.at[y, c], p_s, p_r, pc_s, pc_r)
     w_step(0)
     w_step(1)
 
-    def c_copy(j, s, d):
-        rows = pl.ds(aligned(s * 64, 64), 64)
+    def way_of(s):
+        return s // 2
+
+    def ahead(way):
+        return turn(z, 1 + 2 * way)
+
+    def behind(way):
+        return turn(z, 3 - 2 * way)
+
+    def piece(s):
+        return pl.ds(aligned(s * 64, 64), 64)
+
+    def hop_copy(j, s):
+        way = way_of(s)
         return remote(
-            cs.at[j, turn(z, d), rows, :],
-            cr.at[d - 1, j, rows, :],
-            c_s.at[d - 1, j],
-            c_r.at[d - 1, j],
-            z_peer(d),
+            cs.at[j, turn(z, 2), piece(s), :],
+            hop.at[j, piece(s), :],
+            h_s.at[j, s],
+            h_r.at[j, s],
+            device(x, y, ahead(way), c),
         )
 
-    def c_all(j, d):
+    def c_copy(j, s, way):
+        there = ahead(way)
         return remote(
-            cs.at[j, turn(z, d)], cr.at[d - 1, j], c_s.at[d - 1, j], c_r.at[d - 1, j], mate
+            cs.at[j, there, piece(s), :],
+            cr.at[way, j, piece(s), :],
+            c_s.at[way, j],
+            c_r.at[way, j],
+            device(x, y, there, c),
         )
+
+    def c_all(j, way):
+        return remote(
+            cs.at[j, ahead(way)], cr.at[way, j], c_s.at[way, j], c_r.at[way, j], mate
+        )
+
+    def combine(j, i):
+        s = turn(y, 4 - near(i))
+        way = way_of(s)
+        hop_copy(j, s).wait_recv()
+        both = cs[j, ahead(way), piece(s), :].astype(f32) + hop[j, piece(s), :].astype(f32)
+        cs[j, ahead(way), piece(s), :] = both.astype(bf16)
+        c_copy(j, s, way).start()
 
     def t_copy(j, d):
         block = att.at[z, :, pl.ds(aligned(j * 128, 128), 128)]
         return remote(block, block, t_s.at[d], t_r.at[d], z_peer(d))
 
     def attend_head(j):
-        for d in range(1, 4):
-            c_all(j, d).wait_recv()
-        projected = cs[j, z].astype(f32)
-        for d in range(3):
-            projected = projected + cr[d, j].astype(f32)
+        c_all(j, 0).wait_recv()
+        c_all(j, 1).wait_recv()
+        projected = cs[j, z].astype(f32) + cr[0, j].astype(f32) + cr[1, j].astype(f32)
         queries = norm(projected[:, 0:128], qg_ref[...]).astype(bf16)
         keys = norm(projected[:, 128:256], kg_ref[...]).astype(bf16)
         mixed = attention(queries, keys, projected[:, 256:384].astype(bf16), 128 ** (-0.5))
@@ -266,32 +296,85 @@
         for d in (1, 3, 2):
             t_copy(j, d).start()
 
-    def ew_part(owner, part):
-        return ew.at[owner, pl.ds(aligned(part * 48, 16), 48), :]
+    def ew_half(owner, half):
+        return ew.at[owner, pl.ds(aligned(half * 192, 192), 192), :]
 
     def ex_copy(d):
-        block = ew_part(x, row)
+        block = ew_half(x, c)
         return remote(block, block, ex_s.at[d], ex_r.at[d], x_peer(d))
 
     def ex_got(d):
-        block = ew_part(turn(x, 4 - d), row)
+        block = ew_half(turn(x, 4 - d), c)
         return remote(block, block, ex_s.at[d], ex_r.at[d], mate)
 
-    def ey_copy(d, e):
-        block = ew_part(turn(x, 4 - d), row)
-        return remote(block, block, ey_s.at[d, e], ey_r.at[d, e], y_peer(e))
-
-    def ey_got(d, e):
-        block = ew_part(turn(x, 4 - d), turn(y, 4 - e) * 2 + c)
-        return remote(block, block, ey_s.at[d, e], ey_r.at[d, e], mate)
-
-    def ec_copy(d, e):
-        block = ew_part(turn(x, 4 - d), turn(y, 4 - e) * 2 + c)
-        return remote(block, block, ec_s.at[d, e], ec_r.at[d, e], mate)
-
-    def ec_got(d, e):
-        block = ew_part(turn(x, 4 - d), turn(y, 4 - e) * 2 + 1 - c)
-        return remote(block, block, ec_s.at[d, e], ec_r.at[d, e], mate)
+    def ec_copy(d):
+        block = ew_half(turn(x, 4 - d), c)
+        return remote(block, block, ec_s.at[d], ec_r.at[d], mate)
+
+    def ec_got(d):
+        block = ew_half(turn(x, 4 - d), 1 - c)
+        return remote(block, block, ec_s.at[d], ec_r.at[d], mate)
+
+    first_half = lax.broadcasted_iota(jnp.int32, (256, 128), 1) < 64
+
+    def decoder_heads(tokens):
+        normed = norm(tokens, dg_ref[...]).astype(bf16)
+        made = jnp.dot(normed, dpw[...], preferred_element_type=f32)
+        queries = jnp.concatenate([made[:, 0:64], made[:, 192:256]], axis=1)
+        keys = jnp.concatenate([made[:, 64:128], made[:, 256:320]], axis=1)
+        values = jnp.concatenate([made[:, 128:192], made[:, 320:384]], axis=1)
+        query_gain = jnp.concatenate([dqg_ref[...], dqg_ref[...]], axis=1)
+        key_gain = jnp.concatenate([dkg_ref[...], dkg_ref[...]], axis=1)
+        queries = pair_norm(queries, query_gain)
+        one = jnp.where(first_half, queries, 0.0).astype(bf16)
+        two = jnp.where(first_half, 0.0, queries).astype(bf16)
+        return one, two, pair_norm(keys, key_gain).astype(bf16), values
+
+    def decoder_mix(queries, keys, values):
+        scores = lax.dot_general(queries, keys, LAST, preferred_element_type=f32)
+        weights = jnp.exp(scores * 64 ** (-0.5)).astype(bf16)
+        return jnp.dot(weights, values, preferred_element_type=f32)
+
+    def block_rows(i):
+        return pl.ds(aligned(i * 256, 256), 256)
+
+    def hidden_heads(i):
+        rows = block_rows(i)
+        positions = lax.broadcasted_iota(jnp.int32, (256, 256), 0) + i * 256
+        select = jnp.where(positions == vi_ref[...], 1.0, 0.0)
+        sel[rows, :] = select.astype(bf16)
+        hidden = 1.0 - jnp.sum(select, axis=1, keepdims=True)
+        tokens = hidden * mask_ref[...] + pos[i].reshape(256, DD).astype(f32) + scr[0:1, :]
+
+        @pl.when(i == y)
+        def _():
+            tok[...] = tokens
+
+        one, two, keys, values = decoder_heads(tokens)
+        dq[0, rows, :] = one
+        dq[1, rows, :] = two
+        dk[rows, :] = keys
+        dv[rows, 0:128] = (values * hidden).astype(bf16)
+        dv[rows, 128:256] = jnp.broadcast_to(hidden, (256, 128)).astype(bf16)
+
+    def hidden_mix(i):
+        rows = block_rows(i)
+        for h in range(2):
+            base[h, rows, :] = decoder_mix(dq[h, rows, :], dk[...], dv[...])
+
+    def visible_base():
+        places = jnp.broadcast_to(vi_ref[...].astype(f32), (8, 256))
+        places = jnp.transpose(places)[:, 0:1].astype(jnp.int32)
+        positions = lax.broadcasted_iota(jnp.int32, (256, 1024), 1)
+        select = jnp.where(positions == places, 1.0, 0.0).astype(bf16)
+        chosen = jnp.dot(select, pos[...].reshape(1024, DD), preferred_element_type=f32)
+        tokv[...] = chosen + scr[0:1, :]
+
+    ids = lax.broadcasted_iota(jnp.int32, script_ref.shape, 0)
+    scripted = jnp.sum(
+        jnp.where(ids == si_ref[...], script_ref[...].astype(f32), 0.0), axis=0, keepdims=True
+    )
+    scr[...] = jnp.broadcast_to(scripted, (8, DD))
 
     @pl.loop(0, HEADS_OWN)
     def _(j):
@@ -320,40 +403,57 @@
                     first = core * 128 + image * 32
                     rows = pl.ds(aligned(s * 64 + core * 32, 32), 32)
                     cs[j, image, rows, :] = product[first : first + 32]
-            for d in (1, 3, 2):
-                c_copy(j, s, d).start()
-
-        @pl.when(j == 1)
-        def _():
-            fetches[2].wait()
-            fetches[3].wait()
-            spread_rows(pos.at[y, c], p_s, p_r, pc_s, pc_r)
-            for d in (1, 3, 2):
-                ex_copy(d).start()
-
-        @pl.when(j == 3)
+            hop_copy(j, s).start()
+            c_copy(j, s, 1 - way_of(s)).start()
+
+            @pl.when((j == 0) & (i > 0))
+            def _():
+                combine(0, i - 1)
+
+        @pl.when(j == 0)
+        def _():
+            combine(0, 3)
+
+        @pl.when(j == 2)
         def _():
             for e in (1, 3, 2):
                 got = pos.at[turn(y, 4 - e), c]
                 remote(got, got, p_s.at[e], p_r.at[e], mate).wait_recv()
                 remote(got, got, pc_s.at[e], pc_r.at[e], mate).start()
-            for d in (1, 3, 2):
-                ex_got(d).wait_recv()
-                for e in (1, 3, 2):
-                    ey_copy(d, e).start()
-                ec_copy(d, 0).start()
 
         @pl.when(j > 0)
         def _():
             attend_head(j - 1)
 
+            @pl.loop(0, 4)
+            def _(i):
+                combine(j, i)
+
         w_step(j + 2)
 
+        @pl.when(j == 3)
+        def _():
+            fetches[4].wait()
+            for e in range(4):
+                got = pos.at[turn(y, 4 - e), 1 - c]
+                remote(got, got, pc_s.at[e], pc_r.at[e], mate).wait_recv()
+
+        @pl.when((j == 3) | (j == 4))
+        def _():
+            @pl.loop(0, 2)
+            def _(i):
+                hidden_heads((j - 3) * 2 + i)
+
+    fetches[2].wait()
+    for d in (1, 3, 2):
+        ex_copy(d).start()
+
+    @pl.loop(0, 4)
+    def _(i):
+        hidden_mix(i)
+
+    visible_base()
     attend_head(HEADS_OWN - 1)
-    for e in (1, 3, 2):
-        for d in (1, 3, 2):
-            ey_got(d, e).wait_recv()
-            ec_copy(d, e).start()
     for d in (1, 3, 2):
         whole = att.at[turn(z, 4 - d)]
         remote(whole, whole, t_s.at[d], t_r.at[d], mate).wait_recv()
@@ -428,6 +528,9 @@
         es[there] = block.astype(bf16).reshape(4, 32, 384)
         total = total + jnp.sum(block, axis=-1, keepdims=True)
         square = square + jnp.sum(block * block, axis=-1, keepdims=True)
+    for d in (1, 3, 2):
+        ex_got(d).wait_recv()
+        ec_copy(d).start()
     average, rate = share_stats(1, total, square)
     for g in range(4):
         block = (res[g] - average) * rate * gains[g, 1:2, :]
@@ -437,8 +540,7 @@
     enc_ref[pl.ds(x * 4, 4)] = es[x]
 
     for d in (1, 3, 2):
-        for e in range(4):
-            ec_got(d, e).wait_recv()
+        ec_got(d).wait_recv()
     product = jnp.dot(en[...], ew[...].reshape(1536, DD), preferred_element_type=f32)
     eo[...] = product.astype(bf16).reshape(4, 32, DD)
 
@@ -460,44 +562,15 @@
     for k in (4, 5, 2, 3, 6, 7, 1):
         vis_copy(k).start()
 
-    ids = lax.broadcasted_iota(jnp.int32, script_ref.shape, 0)
-    scripted = jnp.sum(
-        jnp.where(ids == si_ref[...], script_ref[...].astype(f32), 0.0), axis=0, keepdims=True
-    )
-    fetches[4].wait()
-    for e in range(4):
-        got = pos.at[turn(y, 4 - e), 1 - c]
-        remote(got, got, pc_s.at[e], pc_r.at[e], mate).wait_recv()
-    dv[:, 128:256] = jnp.ones((1024, 128), bf16)
     for k in range(1, 8):
         block = vis.at[row_from(k // 2, k % 2)]
         remote(block, block, v_s.at[k], v_r.at[k], mate).wait_recv()
-    query_gain = jnp.concatenate([dqg_ref[...], dqg_ref[...]], axis=1)
-    key_gain = jnp.concatenate([dkg_ref[...], dkg_ref[...]], axis=1)
-
-    @pl.loop(0, 4)
-    def _(i):
-        rows = pl.ds(aligned(i * 256, 256), 256)
-        positions = lax.broadcasted_iota(jnp.int32, (256, 256), 0) + i * 256
-        select = jnp.where(positions == vi_ref[...], 1.0, 0.0)
-        present = jnp.sum(select, axis=1, keepdims=True)
-        tokens = jnp.dot(
-            select.astype(bf16), vis[...].reshape(256, DD), preferred_element_type=f32
-        )
-        tokens = tokens + (1.0 - present) * mask_ref[...]
-        tokens = tokens + pos[i].reshape(256, DD).astype(f32) + scripted
-        tok[rows, :] = tokens
-        normed = norm(tokens, dg_ref[...]).astype(bf16)
-        made = jnp.dot(normed, dpw[...], preferred_element_type=f32)
-        queries = jnp.concatenate([made[:, 0:64], made[:, 192:256]], axis=1)
-        keys = jnp.concatenate([made[:, 64:128], made[:, 256:320]], axis=1)
-        values = jnp.concatenate([made[:, 128:192], made[:, 320:384]], axis=1)
-        queries = pair_norm(queries, query_gain)
-        first = lax.broadcasted_iota(jnp.int32, queries.shape, 1) < 64
-        dq[0, rows, :] = jnp.where(first, queries, 0.0).astype(bf16)
-        dq[1, rows, :] = jnp.where(first, 0.0, queries).astype(bf16)
-        dk[rows, :] = pair_norm(keys, key_gain).astype(bf16)
-        dv[rows, 0:128] = values.astype(bf16)
+    one, two, keys, values = decoder_heads(vis[...].reshape(256, DD).astype(f32) + tokv[...])
+    vq[0] = one
+    vq[1] = two
+    vk[...] = keys
+    vv[:, 0:128] = values.astype(bf16)
+    vv[:, 128:256] = jnp.ones((256, 128), bf16)
 
     def mix_copy(e, m):
         owner = turn(y, e) * 2 + c + m - 2 * c * m
@@ -508,19 +581,29 @@
         block = da.at[:, pl.ds(aligned(row_from(e, m) * 128, 128), 128)]
         return remote(block, block, d_s.at[e, m], d_r.at[e, m], mate)
 
+    def finish(both):
+        one = both[0][:, 0:128] / both[0][:, 128:256]
+        two = both[1][:, 0:128] / both[1][:, 128:256]
+        return jnp.where(first_half, one, two).astype(bf16)
+
+    visible = finish(
+        [
+            decoder_mix(vq[h], dk[...], dv[...]) + decoder_mix(vq[h], vk[...], vv[...])
+            for h in range(2)
+        ]
+    )
+
     @pl.loop(0, 4)
     def _(i):
         e = near(3 - i)
         there = turn(y, e)
-        rows = pl.ds(aligned(there * 256, 256), 256)
-        mixtures = []
-        for h in range(2):
-            scores = lax.dot_general(dq[h, rows, :], dk[...], LAST, preferred_element_type=f32)
-            weights = jnp.exp(scores * 64 ** (-0.5)).astype(bf16)
-            both = jnp.dot(weights, dv[...], preferred_element_type=f32)
-            mixtures.append(both[:, 0:128] / both[:, 128:256])
-        first = lax.broadcasted_iota(jnp.int32, (256, 128), 1) < 64
-        mixed = jnp.where(first, mixtures[0], mixtures[1]).astype(bf16)
+        rows = block_rows(there)
+        mixed = finish(
+            [base[h, rows, :] + decoder_mix(dq[h, rows, :], vk[...], vv[...]) for h in range(2)]
+        )
+        placed = jnp.dot(sel[rows, :], visible, preferred_element_type=f32)
+        hidden = dv[rows, 128:256].astype(f32) > 0.5
+        mixed = jnp.where(hidden, mixed.astype(f32), placed).astype(bf16)
         dm[there * 2] = mixed[0:128]
         dm[there * 2 + 1] = mixed[128:256]
 
@@ -535,9 +618,12 @@
     fetches[6].wait()
     for k in range(1, 8):
         mix_got(k // 2, k % 2).wait_recv()
-    decoded = tok[pl.ds(aligned(row * 128, 128), 128), :] + jnp.dot(
-        da[...], dow[...], preferred_element_type=f32
+    tokens = tok[pl.ds(aligned(c * 128, 128), 128), :] + jnp.dot(
+        sel[pl.ds(aligned(row * 128, 128), 128), :],
+        vis[...].reshape(256, DD),
+        preferred_element_type=f32,
     )
+    decoded = tokens + jnp.dot(da[...], dow[...], preferred_element_type=f32)
     normed = norm(decoded, hg_ref[...]).astype(bf16)
     predicted = jnp.dot(normed, pxw[...], preferred_element_type=f32) + pb_ref[...]
     pred_ref[0] = predicted.astype(bf16)
@@ -554,10 +640,7 @@
         eb_copy(d).wait_send()
         whole = att.at[z]
         remote(whole, whole, t_s.at[d], t_r.at[d], mate).wait_send()
-        ec_copy(d, 0).wait_send()
-        for e in range(1, 4):
-            ey_copy(d, e).wait_send()
-            ec_copy(d, e).wait_send()
+        ec_copy(d).wait_send()
     for e in range(4):
         for block, s_y, r_y, s_c, r_c in (
             (a, ay_s, ay_r, ac_s, ac_r),
@@ -583,8 +666,12 @@
 
     @pl.loop(0, HEADS_OWN)
     def _(j):
-        for d in range(1, 4):
-            c_all(j, d).wait_send()
+        for way in range(2):
+            c_all(j, way).wait_send()
+
+        @pl.loop(0, 4)
+        def _(s):
+            hop_copy(j, s).wait_send()
 
 
 VMEM = pl.BlockSpec(memory_space=pltpu.VMEM)
@@ -638,7 +725,8 @@
             pltpu.VMEM((4, 2, 128, 1536), bf16),
             pltpu.VMEM((CHUNKS, 1536, 384), bf16),
             pltpu.VMEM((HEADS_OWN, 4, 256, 384), bf16),
-            pltpu.VMEM((3, HEADS_OWN, 256, 384), bf16),
+            pltpu.VMEM((2, HEADS_OWN, 256, 384), bf16),
+            pltpu.VMEM((HEADS_OWN, 256, 384), bf16),
             pltpu.VMEM((4, 256, 768), bf16),
             pltpu.VMEM((4, 2, 4, 128, 384), bf16),
             pltpu.VMEM((4, 4, 128, 384), bf16),
@@ -654,10 +742,17 @@
             pltpu.VMEM((4, 32, DD), bf16),
             pltpu.VMEM((3, 32, DD), bf16),
             pltpu.VMEM((8, 32, DD), bf16),
-            pltpu.VMEM((1024, DD), f32),
+            pltpu.VMEM((8, DD), f32),
+            pltpu.VMEM((1024, 256), bf16),
+            pltpu.VMEM((256, DD), f32),
+            pltpu.VMEM((256, DD), f32),
             pltpu.VMEM((2, 1024, 128), bf16),
             pltpu.VMEM((1024, 128), bf16),
             pltpu.VMEM((1024, 256), bf16),
+            pltpu.VMEM((2, 1024, 256), f32),
+            pltpu.VMEM((2, 256, 128), bf16),
+            pltpu.VMEM((256, 128), bf16),
+            pltpu.VMEM((256, 256), bf16),
             pltpu.VMEM((8, 128, 128), bf16),
             pltpu.VMEM((128, DD), bf16),
             dma((7,)),
@@ -669,13 +764,13 @@
             *two,
             dma((2, CHUNKS)), dma((2, CHUNKS)),
             dma((2, CHUNKS)), dma((2, CHUNKS)),
-            dma((3, HEADS_OWN)), dma((3, HEADS_OWN)),
-            *two,
-            *two,
-            *two,
-            *two,
-            dma((4, 4)), dma((4, 4)),
-            dma((4, 4)), dma((4, 4)),
+            dma((HEADS_OWN, 4)), dma((HEADS_OWN, 4)),
+            dma((2, HEADS_OWN)), dma((2, HEADS_OWN)),
+            *two,
+            *two,
+            *two,
+            *two,
+            *two,
             *two,
             dma((4, 4)), dma((4, 4)),
             *two,

time: 171 us -> 167 us (0.977)
  Pallas kernels: 163 us -> 158 us
    pallas_call x1, Pallas kernels: 163 us -> 158 us  [local(): pl.pallas_call(kernel, out_shape=(jax.ShapeDtypeStruct((16, 32, 384), bf1...]
where the time goes in v3:
time: 167 us; the launch traced here: 166 us
  Pallas kernels  158 us (95%)
  local copies, waits for them, and re-layouts  7.17 us (4%)
    pallas_call x1, Pallas kernels, local(): pl.pallas_call(kernel, out_shape=(jax.ShapeDtypeStruct((16, 32, 384), bf1...  158 us
    reshape x3, local copies, waits for them, and re-layouts, flat(): return vector.reshape(1, -1)  3.77 us
    unnamed x2, local copies, waits for them, and re-layouts  3.4 us

profile of v3, /device:TPU:1, one launch (start us, length us, event | category | flops | bytes accessed | tf_op | source)
XLA Modules:
  0.0 166.2 jit_solution(10639210686880445872)
XLA Ops:
  1.3 1.2 reshape.40.ig_ref
  2.5 1.3 reshape.43.fg_ref
  3.8 1.3 reshape.50.pb_ref
  5.0 157.8 %masked_patches.1 = (bf16[16,32,384]{2,1,0:T(8,128)(2,1)}, bf16[1,128,768]{2,1,0:T(8,128)(2,1)}) custom-call(bf16[16,32,384]{2,1,0:T(8,128)(2,1)} %x_ref.1, f32[1,384]{1,0:T(1,128)} %reshape.40.ig_ref, bf16[384,2304]{1,0:T(8,128)(2,1)} %w_ref.1, f32[1,128]{1,0:T(1,128)} %bitcast.14, f32[1,128]{1,0:T(1,128)} %bitcast.15, bf16[768,384]{1,0:T(8,128)(2,1)} %wo_ref.1, ...), custom_call_target="tpu_custom_call" | custom-call | tf_op jit(solution)/shard_map/masked_patches/pallas_call | solution.py:710
  162.8 1.8 %copy.27 = bf16[16,32,384]{2,1,0:T(8,128)(2,1)} copy(bf16[16,32,384]{2,1,0:T(8,128)(2,1)} %get-tuple-element.4) | data formatting | bytes 786432
  164.6 1.6 copy.28

commit v4 on v3

--- a/solution.py
+++ b/solution.py
@@ -8,7 +8,6 @@
 D = 6144
 DD = 1024
 HEADS_OWN = 6
-CHUNKS = 8
 MESH = pl.DeviceIdType.MESH
 bf16 = jnp.bfloat16
 f32 = jnp.float32
@@ -76,9 +75,9 @@
     x_ref, ig_ref, w_ref, qg_ref, kg_ref, wo_ref, fg_ref, ew_ref, eb_ref, mask_ref, pos_ref,
     script_ref, dg_ref, dp_ref, dqg_ref, dkg_ref, do_ref, hg_ref, pw_ref, pb_ref, vi_ref, si_ref,
     enc_ref, pred_ref,
-    gains, raw, stats, a, w, cs, cr, hop, att, po, pr, yr, res, en, es, ew, pos, dpw, dow, pxw,
+    gains, fgains, raw, own, stats, a, w, wo, cs, cr, hop, att, po, pr, yr, res, en, es, ew, pos, dpw, dow, pxw,
     eo, er, vis, scr, sel, tok, tokv, dq, dk, dv, base, vq, vk, vv, dm, da,
-    l_s, w_s, g_s, g_r, x_s, x_r, st_s, st_r, ay_s, ay_r, ac_s, ac_r, wn_s, wn_r, wf_s, wf_r,
+    l_s, w_s, g_s, g_r, f_s, f_r, x_s, x_r, o_s, o_r, wo_s, wo_r, st_s, st_r, ay_s, ay_r, ac_s, ac_r, wn_s, wn_r, wf_s, wf_r,
     h_s, h_r, c_s, c_r, t_s, t_r, p_s, p_r, pc_s, pc_r, ex_s, ex_r, ec_s, ec_r,
     m_s, m_r, y_s, y_r, en_s, en_r, eb_s, eb_r, v_s, v_r, d_s, d_r,
 ):
@@ -115,22 +114,18 @@
         w_fetch(j).start()
 
     fetches = [
-        pltpu.make_async_copy(wo_ref.at[0:384], w_block(6, x, 0, 384), l_s.at[0]),
-        pltpu.make_async_copy(wo_ref.at[384:768], w_block(7, x, 0, 384), l_s.at[1]),
-        pltpu.make_async_copy(ew_ref, ew.at[x], l_s.at[2]),
-        pltpu.make_async_copy(pos_ref, pos.at[y, c], l_s.at[3]),
+        pltpu.make_async_copy(wo_ref, wo.at[z], l_s.at[0]),
+        pltpu.make_async_copy(ew_ref, ew.at[z], l_s.at[1]),
+        pltpu.make_async_copy(pos_ref, pos.at[y, c], l_s.at[2]),
         pltpu.make_async_copy(
-            dp_ref.at[:, pl.ds(aligned(row * 384, 128), 384)], dpw, l_s.at[4]
+            dp_ref.at[:, pl.ds(aligned(row * 384, 128), 384)], dpw, l_s.at[3]
         ),
-        pltpu.make_async_copy(do_ref, dow, l_s.at[5]),
-        pltpu.make_async_copy(pw_ref, pxw, l_s.at[6]),
+        pltpu.make_async_copy(do_ref, dow, l_s.at[4]),
+        pltpu.make_async_copy(pw_ref, pxw, l_s.at[5]),
     ]
-    for fetch in fetches:
-        fetch.start()
-
-    first_row = lax.broadcasted_iota(jnp.int32, (8, 384), 0) == 0
-    gains[x] = jnp.where(first_row, ig_ref[...], fg_ref[...])
-    raw[x] = x_ref[pl.ds(x * 4, 4)]
+
+    gains[x] = jnp.broadcast_to(ig_ref[...], (8, 384))
+    fgains[z] = jnp.broadcast_to(fg_ref[...], (8, 384))
 
     barrier = pltpu.get_barrier_semaphore()
     peers = (
@@ -143,15 +138,27 @@
     pl.semaphore_wait(barrier, len(peers))
 
     def raw_copy(d):
-        there = turn(x, d)
-        return remote(x_ref.at[pl.ds(there * 4, 4)], raw.at[x], x_s.at[d], x_r.at[d], x_peer(d))
+        return remote(x_ref.at[turn(x, d)], raw.at[x], x_s.at[d], x_r.at[d], x_peer(d))
 
     def gain_copy(d):
         return remote(gains.at[x], gains.at[x], g_s.at[d], g_r.at[d], x_peer(d))
 
+    def own_copy(d):
+        return remote(x_ref.at[:, turn(z, d)], own.at[z], o_s.at[d], o_r.at[d], z_peer(d))
+
+    def fgain_copy(d):
+        return remote(fgains.at[z], fgains.at[z], f_s.at[d], f_r.at[d], z_peer(d))
+
+    def wo_copy(d):
+        return remote(wo.at[z], wo.at[z], wo_s.at[d], wo_r.at[d], z_peer(d))
+
     for d in (1, 3, 2):
         gain_copy(d).start()
         raw_copy(d).start()
+    for fetch in fetches:
+        fetch.start()
+    raw[x] = x_ref[x]
+    own[z] = x_ref[:, z]
 
     def w_send(j, way):
         block = w_block(j, x, 0, 384)
@@ -172,6 +179,7 @@
         return remote(block, block, wf_s.at[way, j], wf_r.at[way, j], mate)
 
     def w_start(j):
+        w_fetch(j).wait()
         w_send(j, 0).start()
         w_send(j, 1).start()
 
@@ -181,30 +189,26 @@
         w_got(j, 1).wait_recv()
         w_forward(j, 1).start()
 
-        @pl.when(j + 2 < CHUNKS)
+        @pl.when(j + 2 < HEADS_OWN)
         def _():
             w_start(j + 2)
 
-    @pl.loop(0, HEADS_OWN)
-    def _(j):
-        w_fetch(j).wait()
-
-    fetches[0].wait()
-    fetches[1].wait()
     w_start(0)
     w_start(1)
 
     def stat_copy(n, d, owner):
         block = stats.at[n, owner]
-        return remote(block, block, st_s.at[n, d], st_r.at[n, d], z_peer(d))
+        peer = z_peer(d) if n == 0 else x_peer(d)
+        return remote(block, block, st_s.at[n, d], st_r.at[n, d], peer)
 
     def share_stats(n, total, square):
         lane = lax.broadcasted_iota(jnp.int32, (128, 128), 1)
-        stats[n, z] = jnp.transpose(jnp.where(lane == 0, total, square))[0:8]
+        me = z if n == 0 else x
+        stats[n, me] = jnp.transpose(jnp.where(lane == 0, total, square))[0:8]
         for d in (1, 3, 2):
-            stat_copy(n, d, z).start()
+            stat_copy(n, d, me).start()
         for d in (1, 3, 2):
-            stat_copy(n, d, turn(z, 4 - d)).wait_recv()
+            stat_copy(n, d, turn(me, 4 - d)).wait_recv()
         sums = jnp.transpose(jnp.sum(stats[n], axis=0))
         average = sums[:, 0:1] / D
         spread = sums[:, 1:2] / D - average * average
@@ -231,8 +235,13 @@
         remote(block, block, s_c.at[0], r_c.at[0], mate).start()
 
     spread_rows(a.at[y, c], ay_s, ay_r, ac_s, ac_r)
-    fetches[3].wait()
+    fetches[2].wait()
     spread_rows(pos.at[y, c], p_s, p_r, pc_s, pc_r)
+    fetches[0].wait()
+    for d in (1, 3, 2):
+        fgain_copy(d).start()
+        own_copy(d).start()
+        wo_copy(d).start()
     w_step(0)
     w_step(1)
 
@@ -281,9 +290,10 @@
         cs[j, ahead(way), piece(s), :] = both.astype(bf16)
         c_copy(j, s, way).start()
 
-    def t_copy(j, d):
-        block = att.at[z, :, pl.ds(aligned(j * 128, 128), 128)]
-        return remote(block, block, t_s.at[d], t_r.at[d], z_peer(d))
+    def att_send(j, heads):
+        block = att.at[x, :, pl.ds(aligned(j * 128, 128), heads * 128)]
+        for d in (1, 3, 2):
+            remote(block, block, t_s.at[d], t_r.at[d], x_peer(d)).start()
 
     def attend_head(j):
         c_all(j, 0).wait_recv()
@@ -292,27 +302,25 @@
         queries = norm(projected[:, 0:128], qg_ref[...]).astype(bf16)
         keys = norm(projected[:, 128:256], kg_ref[...]).astype(bf16)
         mixed = attention(queries, keys, projected[:, 256:384].astype(bf16), 128 ** (-0.5))
-        att[z, :, pl.ds(aligned(j * 128, 128), 128)] = mixed
-        for d in (1, 3, 2):
-            t_copy(j, d).start()
+        att[x, :, pl.ds(aligned(j * 128, 128), 128)] = mixed
 
     def ew_half(owner, half):
         return ew.at[owner, pl.ds(aligned(half * 192, 192), 192), :]
 
     def ex_copy(d):
-        block = ew_half(x, c)
-        return remote(block, block, ex_s.at[d], ex_r.at[d], x_peer(d))
+        block = ew_half(z, c)
+        return remote(block, block, ex_s.at[d], ex_r.at[d], z_peer(d))
 
     def ex_got(d):
-        block = ew_half(turn(x, 4 - d), c)
+        block = ew_half(turn(z, 4 - d), c)
         return remote(block, block, ex_s.at[d], ex_r.at[d], mate)
 
     def ec_copy(d):
-        block = ew_half(turn(x, 4 - d), c)
+        block = ew_half(turn(z, 4 - d), c)
         return remote(block, block, ec_s.at[d], ec_r.at[d], mate)
 
     def ec_got(d):
-        block = ew_half(turn(x, 4 - d), 1 - c)
+        block = ew_half(turn(z, 4 - d), 1 - c)
         return remote(block, block, ec_s.at[d], ec_r.at[d], mate)
 
     first_half = lax.broadcasted_iota(jnp.int32, (256, 128), 1) < 64
@@ -429,11 +437,21 @@
             def _(i):
                 combine(j, i)
 
-        w_step(j + 2)
+        @pl.when(j + 2 < HEADS_OWN)
+        def _():
+            w_step(j + 2)
 
         @pl.when(j == 3)
         def _():
-            fetches[4].wait()
+            att_send(0, 3)
+
+        @pl.when(j > 3)
+        def _():
+            att_send(j - 1, 1)
+
+        @pl.when(j == 3)
+        def _():
+            fetches[3].wait()
             for e in range(4):
                 got = pos.at[turn(y, 4 - e), 1 - c]
                 remote(got, got, pc_s.at[e], pc_r.at[e], mate).wait_recv()
@@ -444,7 +462,7 @@
             def _(i):
                 hidden_heads((j - 3) * 2 + i)
 
-    fetches[2].wait()
+    fetches[1].wait()
     for d in (1, 3, 2):
         ex_copy(d).start()
 
@@ -454,12 +472,18 @@
 
     visible_base()
     attend_head(HEADS_OWN - 1)
-    for d in (1, 3, 2):
-        whole = att.at[turn(z, 4 - d)]
+    att_send(HEADS_OWN - 1, 1)
+    for d in (1, 3, 2):
+        there = turn(z, 4 - d)
+        remote(fgains.at[there], fgains.at[there], f_s.at[d], f_r.at[d], mate).wait_recv()
+        remote(own.at[there], own.at[there], o_s.at[d], o_r.at[d], mate).wait_recv()
+        remote(wo.at[there], wo.at[there], wo_s.at[d], wo_r.at[d], mate).wait_recv()
+    for d in (1, 3, 2):
+        whole = att.at[turn(x, 4 - d)]
         remote(whole, whole, t_s.at[d], t_r.at[d], mate).wait_recv()
 
     def block_at(i):
-        return turn(x, 4 - near(i))
+        return turn(z, 4 - near(i))
 
     def mate_copy(i):
         there = block_at(i)
@@ -483,16 +507,9 @@
     def _(i):
         there = block_at(i)
 
-        @pl.when(i == 3)
-        def _():
-            for j in (6, 7):
-                w_far(j, 0).wait_recv()
-                w_far(j, 1).wait_recv()
-
-        rows = pl.ds(aligned(there * 384, 384), 384)
-        both = att[...].reshape(1024, 768)
-        product = jnp.dot(both[:, 0:384], w[6, rows, :], preferred_element_type=f32)
-        product = product + jnp.dot(both[:, 384:768], w[7, rows, :], preferred_element_type=f32)
+        product = jnp.dot(
+            att[...].reshape(1024, 768), wo[there], preferred_element_type=f32
+        )
         product = product.astype(bf16)
         for image in range(4):
             for part in range(8):
@@ -508,20 +525,15 @@
 
     reduce_rows(3)
 
-    res[...] = jnp.zeros_like(res)
-
     def enc_copy(d):
-        there = turn(x, d)
-        return remote(
-            es.at[there], enc_ref.at[pl.ds(x * 4, 4)], en_s.at[d], en_r.at[d], x_peer(d)
-        )
+        return remote(es.at[turn(z, d)], enc_ref.at[:, z], en_s.at[d], en_r.at[d], z_peer(d))
 
     total, square = 0.0, 0.0
     for i in range(4):
         there = block_at(i)
         for e in (1, 3, 2):
             y_copy(i, e).wait_recv()
-        block = raw[there].reshape(128, 384).astype(f32) + po[there, c, y].astype(f32)
+        block = own[there].reshape(128, 384).astype(f32) + po[there, c, y].astype(f32)
         for e in range(3):
             block = block + yr[e, there].astype(f32)
         res[there] = block
@@ -533,11 +545,11 @@
         ec_copy(d).start()
     average, rate = share_stats(1, total, square)
     for g in range(4):
-        block = (res[g] - average) * rate * gains[g, 1:2, :]
+        block = (res[g] - average) * rate * fgains[g, 0:1, :]
         en[:, 384 * g : 384 * g + 384] = block.astype(bf16)
     for d in (1, 3, 2):
         enc_copy(d).start()
-    enc_ref[pl.ds(x * 4, 4)] = es[x]
+    enc_ref[:, z] = es[z]
 
     for d in (1, 3, 2):
         ec_got(d).wait_recv()
@@ -545,11 +557,11 @@
     eo[...] = product.astype(bf16).reshape(4, 32, DD)
 
     def eb_copy(d):
-        return remote(eo.at[turn(z, d)], er.at[d - 1], eb_s.at[d], eb_r.at[d], z_peer(d))
+        return remote(eo.at[turn(x, d)], er.at[d - 1], eb_s.at[d], eb_r.at[d], x_peer(d))
 
     for d in (1, 3, 2):
         eb_copy(d).start()
-    embedded = eo[z].astype(f32)
+    embedded = eo[x].astype(f32)
     for d in (1, 3, 2):
         eb_copy(d).wait_recv()
         embedded = embedded + er[d - 1].astype(f32)
@@ -614,8 +626,8 @@
         mix_copy(e, 1).start()
 
     da[:, pl.ds(aligned(row * 128, 128), 128)] = dm[row]
+    fetches[4].wait()
     fetches[5].wait()
-    fetches[6].wait()
     for k in range(1, 8):
         mix_got(k // 2, k % 2).wait_recv()
     tokens = tok[pl.ds(aligned(c * 128, 128), 128), :] + jnp.dot(
@@ -629,16 +641,19 @@
     pred_ref[0] = predicted.astype(bf16)
 
     for d in range(1, 4):
-        block = enc_ref.at[pl.ds(turn(x, 4 - d) * 4, 4)]
+        block = enc_ref.at[:, turn(z, 4 - d)]
         remote(block, block, en_s.at[d], en_r.at[d], mate).wait_recv()
         enc_copy(d).wait_send()
         gain_copy(d).wait_send()
         raw_copy(d).wait_send()
+        own_copy(d).wait_send()
+        fgain_copy(d).wait_send()
+        wo_copy(d).wait_send()
         stat_copy(0, d, z).wait_send()
-        stat_copy(1, d, z).wait_send()
+        stat_copy(1, d, x).wait_send()
         ex_copy(d).wait_send()
         eb_copy(d).wait_send()
-        whole = att.at[z]
+        whole = att.at[x]
         remote(whole, whole, t_s.at[d], t_r.at[d], mate).wait_send()
         ec_copy(d).wait_send()
     for e in range(4):
@@ -658,7 +673,7 @@
         vis_copy(k).wait_send()
         mix_copy(k // 2, k % 2).wait_send()
 
-    @pl.loop(0, CHUNKS)
+    @pl.loop(0, HEADS_OWN)
     def _(j):
         for way in range(2):
             w_send(j, way).wait_send()
@@ -707,10 +722,10 @@
 
     dma = pltpu.SemaphoreType.DMA
     two = [dma((4,)), dma((4,))]
-    return pl.pallas_call(
+    encoded, predicted = pl.pallas_call(
         kernel,
         out_shape=(
-            jax.ShapeDtypeStruct((16, 32, 384), bf16),
+            jax.ShapeDtypeStruct((4, 4, 32, 384), bf16),
             jax.ShapeDtypeStruct((1, 128, 768), bf16),
         ),
         in_specs=[
@@ -720,10 +735,13 @@
         out_specs=(VMEM, VMEM),
         scratch_shapes=[
             pltpu.VMEM((4, 8, 384), f32),
+            pltpu.VMEM((4, 8, 384), f32),
+            pltpu.VMEM((4, 4, 32, 384), bf16),
             pltpu.VMEM((4, 4, 32, 384), bf16),
             pltpu.VMEM((2, 4, 8, 128), f32),
             pltpu.VMEM((4, 2, 128, 1536), bf16),
-            pltpu.VMEM((CHUNKS, 1536, 384), bf16),
+            pltpu.VMEM((HEADS_OWN, 1536, 384), bf16),
+            pltpu.VMEM((4, 768, 384), bf16),
             pltpu.VMEM((HEADS_OWN, 4, 256, 384), bf16),
             pltpu.VMEM((2, HEADS_OWN, 256, 384), bf16),
             pltpu.VMEM((HEADS_OWN, 256, 384), bf16),
@@ -755,15 +773,18 @@
             pltpu.VMEM((256, 256), bf16),
             pltpu.VMEM((8, 128, 128), bf16),
             pltpu.VMEM((128, DD), bf16),
-            dma((7,)),
+            dma((6,)),
             dma((HEADS_OWN,)),
             *two,
             *two,
+            *two,
+            *two,
+            *two,
             dma((2, 4)), dma((2, 4)),
             *two,
             *two,
-            dma((2, CHUNKS)), dma((2, CHUNKS)),
-            dma((2, CHUNKS)), dma((2, CHUNKS)),
+            dma((2, HEADS_OWN)), dma((2, HEADS_OWN)),
+            dma((2, HEADS_OWN)), dma((2, HEADS_OWN)),
             dma((HEADS_OWN, 4)), dma((HEADS_OWN, 4)),
             dma((2, HEADS_OWN)), dma((2, HEADS_OWN)),
             *two,
@@ -783,12 +804,13 @@
         ),
         name="masked_patches",
     )(
-        visible_patches, flat(input_gain), encoder_project, flat(query_gain), flat(key_gain),
+        visible_patches.reshape(4, 4, 32, 384), flat(input_gain), encoder_project, flat(query_gain), flat(key_gain),
         output_weight, flat(final_gain), embed_weight, flat(embed_bias), flat(mask_token),
         position_embed, script_table, flat(decoder_gain), decoder_project, flat(decoder_query),
         flat(decoder_key), decoder_output, flat(head_gain), pixel_weight, flat(pixel_bias),
         visible_index, flat(script_index),
     )
+    return encoded.reshape(16, 32, 384), predicted
 
 
 def solution(mesh):

time: 167 us -> 175 us (1.048)
  Pallas kernels: 158 us -> 167 us
    pallas_call x1, Pallas kernels: 158 us -> 167 us  [local(): pl.pallas_call(kernel, out_shape=(jax.ShapeDtypeStruct((4, 4, 32, 384), b...]
where the time goes in v4:
time: 175 us
  Pallas kernels  167 us (95%)
  local copies, waits for them, and re-layouts  7.17 us (4%)
    pallas_call x1, Pallas kernels, local(): pl.pallas_call(kernel, out_shape=(jax.ShapeDtypeStruct((4, 4, 32, 384), b...  167 us
    reshape x3, local copies, waits for them, and re-layouts, flat(): return vector.reshape(1, -1)  3.77 us

profile of v4, /device:TPU:1, one launch (start us, length us, event | category | flops | bytes accessed | tf_op | source)
XLA Modules:
  0.0 175.0 jit_solution(16812557826573972961)
XLA Ops:
  1.3 1.2 reshape.47.ig_ref
  2.5 1.3 reshape.50.fg_ref
  3.8 1.3 reshape.57.pb_ref
  5.0 166.5 %masked_patches.1 = (bf16[4,4,32,384]{3,2,1,0:T(8,128)(2,1)}, bf16[1,128,768]{2,1,0:T(8,128)(2,1)}) custom-call(bf16[4,4,32,384]{3,2,1,0:T(8,128)(2,1)} %bitcast.12, f32[1,384]{1,0:T(1,128)} %reshape.47.ig_ref, bf16[384,2304]{1,0:T(8,128)(2,1)} %w_ref.1, f32[1,128]{1,0:T(1,128)} %bitcast.18, f32[1,128]{1,0:T(1,128)} %bitcast.19, bf16[768,384]{1,0:T(8,128)(2,1)} %wo_ref.1, ...), custom_call_target="tpu_custom_call" | custom-call | tf_op jit(solution)/shard_map/masked_patches/pallas_call | solution.py:725
  171.6 1.8 %copy.27 = bf16[16,32,384]{2,1,0:T(8,128)(2,1)} copy(bf16[16,32,384]{2,1,0:T(8,128)(2,1)} %bitcast.13) | data formatting | bytes 786432
  173.4 1.6 copy.28

commit v5 on v4

--- a/solution.py
+++ b/solution.py
@@ -124,8 +124,8 @@
         pltpu.make_async_copy(pw_ref, pxw, l_s.at[5]),
     ]
 
-    gains[x] = jnp.broadcast_to(ig_ref[...], (8, 384))
-    fgains[z] = jnp.broadcast_to(fg_ref[...], (8, 384))
+    gains[x] = jnp.broadcast_to(ig_ref[...].reshape(1, 384), (8, 384))
+    fgains[z] = jnp.broadcast_to(fg_ref[...].reshape(1, 384), (8, 384))
 
     barrier = pltpu.get_barrier_semaphore()
     peers = (
@@ -149,8 +149,9 @@
     def fgain_copy(d):
         return remote(fgains.at[z], fgains.at[z], f_s.at[d], f_r.at[d], z_peer(d))
 
-    def wo_copy(d):
-        return remote(wo.at[z], wo.at[z], wo_s.at[d], wo_r.at[d], z_peer(d))
+    def wo_copy(d, half):
+        block = wo.at[z, 384 * half : 384 * half + 384]
+        return remote(block, block, wo_s.at[half, d], wo_r.at[half, d], z_peer(d))
 
     for d in (1, 3, 2):
         gain_copy(d).start()
@@ -189,12 +190,16 @@
         w_got(j, 1).wait_recv()
         w_forward(j, 1).start()
 
-        @pl.when(j + 2 < HEADS_OWN)
-        def _():
-            w_start(j + 2)
+        @pl.when(j + 3 < HEADS_OWN)
+        def _():
+            w_start(j + 3)
 
     w_start(0)
     w_start(1)
+    w_start(2)
+    fetches[0].wait()
+    wo_copy(1, 0).start()
+    wo_copy(3, 0).start()
 
     def stat_copy(n, d, owner):
         block = stats.at[n, owner]
@@ -237,11 +242,9 @@
     spread_rows(a.at[y, c], ay_s, ay_r, ac_s, ac_r)
     fetches[2].wait()
     spread_rows(pos.at[y, c], p_s, p_r, pc_s, pc_r)
-    fetches[0].wait()
-    for d in (1, 3, 2):
-        fgain_copy(d).start()
-        own_copy(d).start()
-        wo_copy(d).start()
+    wo_copy(2, 0).start()
+    for d in (1, 3, 2):
+        wo_copy(d, 1).start()
     w_step(0)
     w_step(1)
 
@@ -429,13 +432,13 @@
                 remote(got, got, p_s.at[e], p_r.at[e], mate).wait_recv()
                 remote(got, got, pc_s.at[e], pc_r.at[e], mate).start()
 
-        @pl.when(j > 0)
-        def _():
-            attend_head(j - 1)
-
+        @pl.when(j > 1)
+        def _():
             @pl.loop(0, 4)
             def _(i):
-                combine(j, i)
+                combine(j - 1, i)
+
+            attend_head(j - 2)
 
         @pl.when(j + 2 < HEADS_OWN)
         def _():
@@ -443,11 +446,11 @@
 
         @pl.when(j == 3)
         def _():
-            att_send(0, 3)
+            att_send(0, 2)
 
         @pl.when(j > 3)
         def _():
-            att_send(j - 1, 1)
+            att_send(j - 2, 1)
 
         @pl.when(j == 3)
         def _():
@@ -462,11 +465,23 @@
             def _(i):
                 hidden_heads((j - 3) * 2 + i)
 
+    @pl.loop(0, 2)
+    def _(i):
+        hidden_mix(i)
+
+    @pl.loop(0, 4)
+    def _(i):
+        combine(HEADS_OWN - 1, i)
+
+    attend_head(HEADS_OWN - 2)
+    att_send(HEADS_OWN - 2, 1)
     fetches[1].wait()
     for d in (1, 3, 2):
+        fgain_copy(d).start()
+        own_copy(d).start()
         ex_copy(d).start()
 
-    @pl.loop(0, 4)
+    @pl.loop(2, 4)
     def _(i):
         hidden_mix(i)
 
@@ -475,9 +490,9 @@
     att_send(HEADS_OWN - 1, 1)
     for d in (1, 3, 2):
         there = turn(z, 4 - d)
-        remote(fgains.at[there], fgains.at[there], f_s.at[d], f_r.at[d], mate).wait_recv()
-        remote(own.at[there], own.at[there], o_s.at[d], o_r.at[d], mate).wait_recv()
-        remote(wo.at[there], wo.at[there], wo_s.at[d], wo_r.at[d], mate).wait_recv()
+        for half in range(2):
+            block = wo.at[there, 384 * half : 384 * half + 384]
+            remote(block, block, wo_s.at[half, d], wo_r.at[half, d], mate).wait_recv()
     for d in (1, 3, 2):
         whole = att.at[turn(x, 4 - d)]
         remote(whole, whole, t_s.at[d], t_r.at[d], mate).wait_recv()
@@ -528,6 +543,10 @@
     def enc_copy(d):
         return remote(es.at[turn(z, d)], enc_ref.at[:, z], en_s.at[d], en_r.at[d], z_peer(d))
 
+    for d in (1, 3, 2):
+        there = turn(z, 4 - d)
+        remote(fgains.at[there], fgains.at[there], f_s.at[d], f_r.at[d], mate).wait_recv()
+        remote(own.at[there], own.at[there], o_s.at[d], o_r.at[d], mate).wait_recv()
     total, square = 0.0, 0.0
     for i in range(4):
         there = block_at(i)
@@ -637,7 +656,7 @@
     )
     decoded = tokens + jnp.dot(da[...], dow[...], preferred_element_type=f32)
     normed = norm(decoded, hg_ref[...]).astype(bf16)
-    predicted = jnp.dot(normed, pxw[...], preferred_element_type=f32) + pb_ref[...]
+    predicted = jnp.dot(normed, pxw[...], preferred_element_type=f32) + pb_ref[...].reshape(1, 768)
     pred_ref[0] = predicted.astype(bf16)
 
     for d in range(1, 4):
@@ -648,7 +667,8 @@
         raw_copy(d).wait_send()
         own_copy(d).wait_send()
         fgain_copy(d).wait_send()
-        wo_copy(d).wait_send()
+        wo_copy(d, 0).wait_send()
+        wo_copy(d, 1).wait_send()
         stat_copy(0, d, z).wait_send()
         stat_copy(1, d, x).wait_send()
         ex_copy(d).wait_send()
@@ -779,7 +799,7 @@
             *two,
             *two,
             *two,
-            *two,
+            dma((2, 4)), dma((2, 4)),
             dma((2, 4)), dma((2, 4)),
             *two,
             *two,
@@ -804,10 +824,10 @@
         ),
         name="masked_patches",
     )(
-        visible_patches.reshape(4, 4, 32, 384), flat(input_gain), encoder_project, flat(query_gain), flat(key_gain),
-        output_weight, flat(final_gain), embed_weight, flat(embed_bias), flat(mask_token),
+        visible_patches.reshape(4, 4, 32, 384), input_gain, encoder_project, flat(query_gain), flat(key_gain),
+        output_weight, final_gain, embed_weight, flat(embed_bias), flat(mask_token),
         position_embed, script_table, flat(decoder_gain), decoder_project, flat(decoder_query),
-        flat(decoder_key), decoder_output, flat(head_gain), pixel_weight, flat(pixel_bias),
+        flat(decoder_key), decoder_output, flat(head_gain), pixel_weight, pixel_bias,
         visible_index, flat(script_index),
     )
     return encoded.reshape(16, 32, 384), predicted

time: 175 us -> 156 us (0.89)
  Pallas kernels: 167 us -> 151 us
  local copies, waits for them, and re-layouts: 7.17 us -> 3.4 us
    pallas_call x1, Pallas kernels: 167 us -> 151 us  [local(): pl.pallas_call(kernel, out_shape=(jax.ShapeDtypeStruct((4, 4, 32, 384), b...]
    reshape x3 -> x0, local copies, waits for them, and re-layouts: 3.77 us -> none  [flat(): return vector.reshape(1, -1)]
where the time goes in v5:
time: 156 us; the launch traced here: 155 us
  Pallas kernels  151 us (97%)
  local copies, waits for them, and re-layouts  3.4 us (2%)
    pallas_call x1, Pallas kernels, local(): pl.pallas_call(kernel, out_shape=(jax.ShapeDtypeStruct((4, 4, 32, 384), b...  151 us
    unnamed x2, local copies, waits for them, and re-layouts  3.4 us

profile of v5, /device:TPU:1, one launch (start us, length us, event | category | flops | bytes accessed | tf_op | source)
XLA Modules:
  0.0 155.5 jit_solution(4645253296822206790)
XLA Ops:
  1.3 150.8 %masked_patches.1 = (bf16[4,4,32,384]{3,2,1,0:T(8,128)(2,1)}, bf16[1,128,768]{2,1,0:T(8,128)(2,1)}) custom-call(bf16[4,4,32,384]{3,2,1,0:T(8,128)(2,1)} %bitcast.12, f32[384]{0:T(512)} %ig_ref.1, bf16[384,2304]{1,0:T(8,128)(2,1)} %w_ref.1, f32[1,128]{1,0:T(1,128)} %bitcast.18, f32[1,128]{1,0:T(1,128)} %bitcast.19, bf16[768,384]{1,0:T(8,128)(2,1)} %wo_ref.1, ...), custom_call_target="tpu_custom_call" | custom-call | tf_op jit(solution)/shard_map/masked_patches/pallas_call | solution.py:745
  152.1 1.8 %copy.27 = bf16[16,32,384]{2,1,0:T(8,128)(2,1)} copy(bf16[16,32,384]{2,1,0:T(8,128)(2,1)} %bitcast.13) | data formatting | bytes 786432
  153.8 1.6 %copy.28 = bf16[1,128,768]{2,1,0:T(8,128)(2,1)} copy(bf16[1,128,768]{2,1,0:T(8,128)(2,1)} %get-tuple-element.9) | data formatting | bytes 393216

commit v6 on v5

--- a/solution.py
+++ b/solution.py
@@ -75,11 +75,11 @@
     x_ref, ig_ref, w_ref, qg_ref, kg_ref, wo_ref, fg_ref, ew_ref, eb_ref, mask_ref, pos_ref,
     script_ref, dg_ref, dp_ref, dqg_ref, dkg_ref, do_ref, hg_ref, pw_ref, pb_ref, vi_ref, si_ref,
     enc_ref, pred_ref,
-    gains, fgains, raw, own, stats, a, w, wo, cs, cr, hop, att, po, pr, yr, res, en, es, ew, pos, dpw, dow, pxw,
+    gains, fgains, raw, own, stats, a, w, wo, cs, cr, hop, att, po, pr, yr, yhop, res, en, es, ew, pos, dpw, dow, pxw,
     eo, er, vis, scr, sel, tok, tokv, dq, dk, dv, base, vq, vk, vv, dm, da,
     l_s, w_s, g_s, g_r, f_s, f_r, x_s, x_r, o_s, o_r, wo_s, wo_r, st_s, st_r, ay_s, ay_r, ac_s, ac_r, wn_s, wn_r, wf_s, wf_r,
     h_s, h_r, c_s, c_r, t_s, t_r, p_s, p_r, pc_s, pc_r, ex_s, ex_r, ec_s, ec_r,
-    m_s, m_r, y_s, y_r, en_s, en_r, eb_s, eb_r, v_s, v_r, d_s, d_r,
+    m_s, m_r, yh_s, yh_r, y_s, y_r, en_s, en_r, eb_s, eb_r, v_s, v_r, vc_s, vc_r, d_s, d_r,
 ):
     row, col = lax.axis_index("row"), lax.axis_index("col")
     x, y, z, c = col // 4, row // 2, lax.rem(col, 4), lax.rem(row, 2)
@@ -387,8 +387,19 @@
     )
     scr[...] = jnp.broadcast_to(scripted, (8, DD))
 
+    def earlier_heads(j):
+        @pl.loop(0, 4)
+        def _(i):
+            combine(j - 1, i)
+
+        attend_head(j - 2)
+
     @pl.loop(0, HEADS_OWN)
     def _(j):
+        @pl.when(j > 2)
+        def _():
+            earlier_heads(j)
+
         w_far(j, 0).wait_recv()
         w_far(j, 1).wait_recv()
 
@@ -432,13 +443,9 @@
                 remote(got, got, p_s.at[e], p_r.at[e], mate).wait_recv()
                 remote(got, got, pc_s.at[e], pc_r.at[e], mate).start()
 
-        @pl.when(j > 1)
-        def _():
-            @pl.loop(0, 4)
-            def _(i):
-                combine(j - 1, i)
-
-            attend_head(j - 2)
+        @pl.when(j == 2)
+        def _():
+            earlier_heads(j)
 
         @pl.when(j + 2 < HEADS_OWN)
         def _():
@@ -504,19 +511,55 @@
         there = block_at(i)
         return remote(po.at[there, 1 - c], pr.at[there], m_s.at[i], m_r.at[i], mate)
 
-    def y_copy(i, e):
+    def y_ahead(way):
+        return turn(y, 1 + 2 * way)
+
+    def half(way):
+        return slice(64 * way, 64 * way + 64)
+
+    def y_hop(i, way):
         there = block_at(i)
         return remote(
-            po.at[there, c, turn(y, e)], yr.at[e - 1, there], y_s.at[e, i], y_r.at[e, i], y_peer(e)
+            po.at[there, c, turn(y, 2), half(way)],
+            yhop.at[there, half(way)],
+            yh_s.at[way, i],
+            yh_r.at[way, i],
+            device(x, y_ahead(way), z, c),
         )
 
-    def reduce_rows(i):
+    def y_copy(i, way, part):
+        there = block_at(i)
+        return remote(
+            po.at[there, c, y_ahead(way), half(part)],
+            yr.at[way, there, half(part)],
+            y_s.at[way, i],
+            y_r.at[way, i],
+            device(x, y_ahead(way), z, c),
+        )
+
+    def y_all(i, way):
+        there = block_at(i)
+        return remote(
+            po.at[there, c, y_ahead(way)], yr.at[way, there], y_s.at[way, i], y_r.at[way, i], mate
+        )
+
+    def reduce_mate(i):
         there = block_at(i)
         mate_copy(i).wait_recv()
         both = po[there, c].astype(f32) + pr[there].astype(f32)
         po[there, c] = both.astype(bf16)
-        for e in (1, 3, 2):
-            y_copy(i, e).start()
+        for way in range(2):
+            y_hop(i, way).start()
+            y_copy(i, way, 1 - way).start()
+
+    def reduce_rows(i):
+        there = block_at(i)
+        for way in range(2):
+            y_hop(i, way).wait_recv()
+            part = po[there, c, y_ahead(way), half(way)].astype(f32)
+            part = part + yhop[there, half(way)].astype(f32)
+            po[there, c, y_ahead(way), half(way)] = part.astype(bf16)
+            y_copy(i, way, way).start()
 
     @pl.loop(0, 4)
     def _(i):
@@ -536,8 +579,14 @@
 
         @pl.when(i > 0)
         def _():
-            reduce_rows(i - 1)
-
+            reduce_mate(i - 1)
+
+        @pl.when(i > 1)
+        def _():
+            reduce_rows(i - 2)
+
+    reduce_mate(3)
+    reduce_rows(2)
     reduce_rows(3)
 
     def enc_copy(d):
@@ -550,11 +599,10 @@
     total, square = 0.0, 0.0
     for i in range(4):
         there = block_at(i)
-        for e in (1, 3, 2):
-            y_copy(i, e).wait_recv()
+        y_all(i, 0).wait_recv()
+        y_all(i, 1).wait_recv()
         block = own[there].reshape(128, 384).astype(f32) + po[there, c, y].astype(f32)
-        for e in range(3):
-            block = block + yr[e, there].astype(f32)
+        block = block + yr[0, there].astype(f32) + yr[1, there].astype(f32)
         res[there] = block
         es[there] = block.astype(bf16).reshape(4, 32, 384)
         total = total + jnp.sum(block, axis=-1, keepdims=True)
@@ -586,16 +634,15 @@
         embedded = embedded + er[d - 1].astype(f32)
     vis[row] = (embedded + eb_ref[...]).astype(bf16)
 
-    def vis_copy(k):
-        block = vis.at[row]
-        return remote(block, block, v_s.at[k], v_r.at[k], row_peer(k // 2, k % 2))
-
-    for k in (4, 5, 2, 3, 6, 7, 1):
-        vis_copy(k).start()
-
-    for k in range(1, 8):
-        block = vis.at[row_from(k // 2, k % 2)]
-        remote(block, block, v_s.at[k], v_r.at[k], mate).wait_recv()
+    spread_rows(vis.at[row], v_s, v_r, vc_s, vc_r)
+
+    for e in (1, 3, 2):
+        got = vis.at[turn(y, 4 - e) * 2 + c]
+        remote(got, got, v_s.at[e], v_r.at[e], mate).wait_recv()
+        remote(got, got, vc_s.at[e], vc_r.at[e], mate).start()
+    for e in range(4):
+        got = vis.at[turn(y, 4 - e) * 2 + 1 - c]
+        remote(got, got, vc_s.at[e], vc_r.at[e], mate).wait_recv()
     one, two, keys, values = decoder_heads(vis[...].reshape(256, DD).astype(f32) + tokv[...])
     vq[0] = one
     vq[1] = two
@@ -687,10 +734,15 @@
             passed = block.at[turn(y, 4 - e), c]
             remote(passed, passed, s_c.at[e], r_c.at[e], mate).wait_send()
         mate_copy(e).wait_send()
-        for i in range(1, 4):
-            y_copy(e, i).wait_send()
+        if e > 0:
+            own_rows = vis.at[row]
+            remote(own_rows, own_rows, v_s.at[e], v_r.at[e], mate).wait_send()
+        passed = vis.at[turn(y, 4 - e) * 2 + c]
+        remote(passed, passed, vc_s.at[e], vc_r.at[e], mate).wait_send()
+        for way in range(2):
+            y_hop(e, way).wait_send()
+            y_all(e, way).wait_send()
     for k in range(1, 8):
-        vis_copy(k).wait_send()
         mix_copy(k // 2, k % 2).wait_send()
 
     @pl.loop(0, HEADS_OWN)
@@ -707,6 +759,17 @@
         @pl.loop(0, 4)
         def _(s):
             hop_copy(j, s).wait_send()
+
+
+def hand_on(enc_ref, pred_ref, enc_out, pred_out, sems):
+    copies = [
+        pltpu.make_async_copy(enc_ref, enc_out, sems.at[0]),
+        pltpu.make_async_copy(pred_ref, pred_out, sems.at[1]),
+    ]
+    for copy in copies:
+        copy.start()
+    for copy in copies:
+        copy.wait()
 
 
 VMEM = pl.BlockSpec(memory_space=pltpu.VMEM)
@@ -768,7 +831,8 @@
             pltpu.VMEM((4, 256, 768), bf16),
             pltpu.VMEM((4, 2, 4, 128, 384), bf16),
             pltpu.VMEM((4, 4, 128, 384), bf16),
-            pltpu.VMEM((3, 4, 128, 384), bf16),
+            pltpu.VMEM((2, 4, 128, 384), bf16),
+            pltpu.VMEM((4, 128, 384), bf16),
             pltpu.VMEM((4, 128, 384), f32),
             pltpu.VMEM((128, 1536), bf16),
             pltpu.VMEM((4, 4, 32, 384), bf16),
@@ -813,10 +877,12 @@
             *two,
             *two,
             *two,
-            dma((4, 4)), dma((4, 4)),
-            *two,
-            *two,
-            dma((8,)), dma((8,)),
+            dma((2, 4)), dma((2, 4)),
+            dma((2, 4)), dma((2, 4)),
+            *two,
+            *two,
+            *two,
+            *two,
             dma((4, 2)), dma((4, 2)),
         ],
         compiler_params=pltpu.CompilerParams(
@@ -830,7 +896,18 @@
         flat(decoder_key), decoder_output, flat(head_gain), pixel_weight, pixel_bias,
         visible_index, flat(script_index),
     )
-    return encoded.reshape(16, 32, 384), predicted
+    encoded = encoded.reshape(16, 32, 384)
+    return pl.pallas_call(
+        hand_on,
+        out_shape=(
+            jax.ShapeDtypeStruct(encoded.shape, bf16),
+            jax.ShapeDtypeStruct(predicted.shape, bf16),
+        ),
+        in_specs=[ANY, ANY],
+        out_specs=(ANY, ANY),
+        scratch_shapes=[dma((2,))],
+        name="hand_on",
+    )(encoded, predicted)
 
 
 def solution(mesh):

time: 156 us -> 165 us (1.058)
  Pallas kernels: 151 us -> 163 us
  local copies, waits for them, and re-layouts: 3.4 us -> 0 us
    pallas_call x0 -> x1, Pallas kernels: none -> 19 us  [local(): pl.pallas_call(hand_on, out_shape=(jax.ShapeDtypeStruct(encoded.shape, bf...]
    pallas_call x1, Pallas kernels: 151 us -> 144 us  [local(): pl.pallas_call(kernel, out_shape=(jax.ShapeDtypeStruct((4, 4, 32, 384), b...]
    unnamed x2 -> x0, local copies, waits for them, and re-layouts: 3.4 us -> none
where the time goes in v6:
time: 165 us
  Pallas kernels  163 us (99%)
    pallas_call x1, Pallas kernels, local(): pl.pallas_call(kernel, out_shape=(jax.ShapeDtypeStruct((4, 4, 32, 384), b...  144 us
    pallas_call x1, Pallas kernels, local(): pl.pallas_call(hand_on, out_shape=(jax.ShapeDtypeStruct(encoded.shape, bf...  19 us

profile of v6, /device:TPU:1, one launch (start us, length us, event | category | flops | bytes accessed | tf_op | source)
XLA Modules:
  0.0 164.8 jit_solution(13191377886561605155)
XLA Ops:
  1.3 144.5 %masked_patches.1 = (bf16[4,4,32,384]{3,2,1,0:T(8,128)(2,1)}, bf16[1,128,768]{2,1,0:T(8,128)(2,1)}) custom-call(bf16[4,4,32,384]{3,2,1,0:T(8,128)(2,1)} %bitcast.12, f32[384]{0:T(512)} %ig_ref.1, bf16[384,2304]{1,0:T(8,128)(2,1)} %w_ref.1, f32[1,128]{1,0:T(1,128)} %bitcast.18, f32[1,128]{1,0:T(1,128)} %bitcast.19, bf16[768,384]{1,0:T(8,128)(2,1)} %wo_ref.1, ...), custom_call_target="tpu_custom_call" | custom-call | tf_op jit(solution)/shard_map/masked_patches/pallas_call | solution.py:808
  145.8 19.0 %hand_on.1 = (bf16[16,32,384]{2,1,0:T(8,128)(2,1)}, bf16[1,128,768]{2,1,0:T(8,128)(2,1)}) custom-call(bf16[16,32,384]{2,1,0:T(8,128)(2,1)} %bitcast.13, bf16[1,128,768]{2,1,0:T(8,128)(2,1)} %get-tuple-element.5.pred_ref), custom_call_target="tpu_custom_call" | custom-call | tf_op jit(solution)/shard_map/hand_on/pallas_call | solution.py:900

commit v7 on v6

--- a/solution.py
+++ b/solution.py
@@ -761,15 +761,9 @@
             hop_copy(j, s).wait_send()
 
 
-def hand_on(enc_ref, pred_ref, enc_out, pred_out, sems):
-    copies = [
-        pltpu.make_async_copy(enc_ref, enc_out, sems.at[0]),
-        pltpu.make_async_copy(pred_ref, pred_out, sems.at[1]),
-    ]
-    for copy in copies:
-        copy.start()
-    for copy in copies:
-        copy.wait()
+def hand_on(enc_ref, pred_ref, enc_out, pred_out):
+    enc_out[...] = enc_ref[...]
+    pred_out[...] = pred_ref[...]
 
 
 VMEM = pl.BlockSpec(memory_space=pltpu.VMEM)
@@ -903,9 +897,8 @@
             jax.ShapeDtypeStruct(encoded.shape, bf16),
             jax.ShapeDtypeStruct(predicted.shape, bf16),
         ),
-        in_specs=[ANY, ANY],
-        out_specs=(ANY, ANY),
-        scratch_shapes=[dma((2,))],
+        in_specs=[VMEM, VMEM],
+        out_specs=(VMEM, VMEM),
         name="hand_on",
     )(encoded, predicted)
 

time: 165 us -> 148 us (0.90)
  Pallas kernels: 163 us -> 146 us
    pallas_call x1, Pallas kernels: 19 us -> 1.89 us  [local(): pl.pallas_call(hand_on, out_shape=(jax.ShapeDtypeStruct(encoded.shape, bf...]
where the time goes in v7:
time: 148 us
  Pallas kernels  146 us (99%)
    pallas_call x1, Pallas kernels, local(): pl.pallas_call(kernel, out_shape=(jax.ShapeDtypeStruct((4, 4, 32, 384), b...  144 us

profile of v7, /device:TPU:1, one launch (start us, length us, event | category | flops | bytes accessed | tf_op | source)
XLA Modules:
  0.0 147.7 jit_solution(10628516531545373586)
XLA Ops:
  1.3 144.5 %masked_patches.1 = (bf16[4,4,32,384]{3,2,1,0:T(8,128)(2,1)}, bf16[1,128,768]{2,1,0:T(8,128)(2,1)}) custom-call(bf16[4,4,32,384]{3,2,1,0:T(8,128)(2,1)} %bitcast.12, f32[384]{0:T(512)} %ig_ref.1, bf16[384,2304]{1,0:T(8,128)(2,1)} %w_ref.1, f32[1,128]{1,0:T(1,128)} %bitcast.18, f32[1,128]{1,0:T(1,128)} %bitcast.19, bf16[768,384]{1,0:T(8,128)(2,1)} %wo_ref.1, ...), custom_call_target="tpu_custom_call" | custom-call | tf_op jit(solution)/shard_map/masked_patches/pallas_call | solution.py:802
  145.8 1.9 %hand_on.1 = (bf16[16,32,384]{2,1,0:T(8,128)(2,1)}, bf16[1,128,768]{2,1,0:T(8,128)(2,1)}) custom-call(bf16[16,32,384]{2,1,0:T(8,128)(2,1)} %bitcast.13, bf16[1,128,768]{2,1,0:T(8,128)(2,1)} %get-tuple-element.5.pred_ref), custom_call_target="tpu_custom_call" | custom-call | tf_op jit(solution)/shard_map/hand_on/pallas_call | solution.py:894

commit v8 on v7

--- a/solution.py
+++ b/solution.py
@@ -8,6 +8,7 @@
 D = 6144
 DD = 1024
 HEADS_OWN = 6
+HEADS_X = 5
 MESH = pl.DeviceIdType.MESH
 bf16 = jnp.bfloat16
 f32 = jnp.float32
@@ -75,9 +76,10 @@
     x_ref, ig_ref, w_ref, qg_ref, kg_ref, wo_ref, fg_ref, ew_ref, eb_ref, mask_ref, pos_ref,
     script_ref, dg_ref, dp_ref, dqg_ref, dkg_ref, do_ref, hg_ref, pw_ref, pb_ref, vi_ref, si_ref,
     enc_ref, pred_ref,
-    gains, fgains, raw, own, stats, a, w, wo, cs, cr, hop, att, po, pr, yr, yhop, res, en, es, ew, pos, dpw, dow, pxw,
+    gains, zgains, raw, own, stats, a, a2, w, wz, wo, cs, cr, hop, att, po, pr, yr, yhop, res, en, es, ew, pos, dpw, dow, pxw,
     eo, er, vis, scr, sel, tok, tokv, dq, dk, dv, base, vq, vk, vv, dm, da,
-    l_s, w_s, g_s, g_r, f_s, f_r, x_s, x_r, o_s, o_r, wo_s, wo_r, st_s, st_r, ay_s, ay_r, ac_s, ac_r, wn_s, wn_r, wf_s, wf_r,
+    l_s, w_s, g_s, g_r, f_s, f_r, x_s, x_r, o_s, o_r, wo_s, wo_r, wz_s, wz_r, st_s, st_r, ay_s, ay_r, ac_s, ac_r,
+    by_s, by_r, bc_s, bc_r, wn_s, wn_r, wf_s, wf_r,
     h_s, h_r, c_s, c_r, t_s, t_r, p_s, p_r, pc_s, pc_r, ex_s, ex_r, ec_s, ec_r,
     m_s, m_r, yh_s, yh_r, y_s, y_r, en_s, en_r, eb_s, eb_r, v_s, v_r, vc_s, vc_r, d_s, d_r,
 ):
@@ -109,7 +111,7 @@
             w_ref.at[:, pl.ds(aligned(j * 384, 128), 384)], w_block(j, x, 0, 384), w_s.at[j]
         )
 
-    @pl.loop(0, HEADS_OWN)
+    @pl.loop(0, HEADS_X)
     def _(j):
         w_fetch(j).start()
 
@@ -122,10 +124,17 @@
         ),
         pltpu.make_async_copy(do_ref, dow, l_s.at[4]),
         pltpu.make_async_copy(pw_ref, pxw, l_s.at[5]),
+        pltpu.make_async_copy(
+            w_ref.at[:, HEADS_X * 384 :], wz.at[pl.ds(aligned(z * 384, 384), 384), :], l_s.at[6]
+        ),
     ]
 
     gains[x] = jnp.broadcast_to(ig_ref[...].reshape(1, 384), (8, 384))
-    fgains[z] = jnp.broadcast_to(fg_ref[...].reshape(1, 384), (8, 384))
+    zgains[z] = jnp.where(
+        lax.broadcasted_iota(jnp.int32, (8, 384), 0) == 0,
+        fg_ref[...].reshape(1, 384),
+        ig_ref[...].reshape(1, 384),
+    )
 
     barrier = pltpu.get_barrier_semaphore()
     peers = (
@@ -146,16 +155,29 @@
     def own_copy(d):
         return remote(x_ref.at[:, turn(z, d)], own.at[z], o_s.at[d], o_r.at[d], z_peer(d))
 
-    def fgain_copy(d):
-        return remote(fgains.at[z], fgains.at[z], f_s.at[d], f_r.at[d], z_peer(d))
-
-    def wo_copy(d, half):
-        block = wo.at[z, 384 * half : 384 * half + 384]
-        return remote(block, block, wo_s.at[half, d], wo_r.at[half, d], z_peer(d))
+    def zgain_copy(d):
+        return remote(zgains.at[z], zgains.at[z], f_s.at[d], f_r.at[d], z_peer(d))
+
+    def wo_copy(d):
+        return remote(wo.at[z], wo.at[z], wo_s.at[d], wo_r.at[d], z_peer(d))
+
+    def wo_got(d):
+        block = wo.at[turn(z, 4 - d)]
+        return remote(block, block, wo_s.at[d], wo_r.at[d], mate)
+
+    def wz_copy(d):
+        block = wz.at[pl.ds(aligned(z * 384, 384), 384), :]
+        return remote(block, block, wz_s.at[d], wz_r.at[d], z_peer(d))
+
+    def wz_got(d):
+        block = wz.at[pl.ds(aligned(turn(z, 4 - d) * 384, 384), 384), :]
+        return remote(block, block, wz_s.at[d], wz_r.at[d], mate)
 
     for d in (1, 3, 2):
         gain_copy(d).start()
         raw_copy(d).start()
+        zgain_copy(d).start()
+        own_copy(d).start()
     for fetch in fetches:
         fetch.start()
     raw[x] = x_ref[x]
@@ -190,28 +212,28 @@
         w_got(j, 1).wait_recv()
         w_forward(j, 1).start()
 
-        @pl.when(j + 3 < HEADS_OWN)
+        @pl.when(j + 3 < HEADS_X)
         def _():
             w_start(j + 3)
 
     w_start(0)
     w_start(1)
     w_start(2)
-    fetches[0].wait()
-    wo_copy(1, 0).start()
-    wo_copy(3, 0).start()
 
     def stat_copy(n, d, owner):
         block = stats.at[n, owner]
         peer = z_peer(d) if n == 0 else x_peer(d)
         return remote(block, block, st_s.at[n, d], st_r.at[n, d], peer)
 
-    def share_stats(n, total, square):
+    def send_stats(n, total, square):
         lane = lax.broadcasted_iota(jnp.int32, (128, 128), 1)
         me = z if n == 0 else x
         stats[n, me] = jnp.transpose(jnp.where(lane == 0, total, square))[0:8]
         for d in (1, 3, 2):
             stat_copy(n, d, me).start()
+
+    def take_stats(n):
+        me = z if n == 0 else x
         for d in (1, 3, 2):
             stat_copy(n, d, turn(me, 4 - d)).wait_recv()
         sums = jnp.transpose(jnp.sum(stats[n], axis=0))
@@ -223,16 +245,24 @@
         there = turn(x, 4 - d)
         remote(gains.at[there], gains.at[there], g_s.at[d], g_r.at[d], mate).wait_recv()
         remote(raw.at[there], raw.at[there], x_s.at[d], x_r.at[d], mate).wait_recv()
-    total, square = 0.0, 0.0
-    for g in range(4):
-        block = raw[g].reshape(128, 384).astype(f32)
-        total = total + jnp.sum(block, axis=-1, keepdims=True)
-        square = square + jnp.sum(block * block, axis=-1, keepdims=True)
-    average, rate = share_stats(0, total, square)
-    for g in range(4):
-        block = raw[g].reshape(128, 384).astype(f32)
-        block = (block - average) * rate * gains[g, 0:1, :]
-        a[y, c, :, 384 * g : 384 * g + 384] = block.astype(bf16)
+
+    def sums_of(blocks):
+        total, square = 0.0, 0.0
+        for g in range(4):
+            block = blocks[g].reshape(128, 384).astype(f32)
+            total = total + jnp.sum(block, axis=-1, keepdims=True)
+            square = square + jnp.sum(block * block, axis=-1, keepdims=True)
+        return total, square
+
+    def input_norm(n, blocks, into, gain_of):
+        average, rate = take_stats(n)
+        for g in range(4):
+            block = blocks[g].reshape(128, 384).astype(f32)
+            block = (block - average) * rate * gain_of(g)
+            into[y, c, :, 384 * g : 384 * g + 384] = block.astype(bf16)
+
+    send_stats(0, *sums_of(raw))
+    input_norm(0, raw, a, lambda g: gains[g, 0:1, :])
 
     def spread_rows(block, s_y, r_y, s_c, r_c):
         for e in (1, 3, 2):
@@ -242,66 +272,86 @@
     spread_rows(a.at[y, c], ay_s, ay_r, ac_s, ac_r)
     fetches[2].wait()
     spread_rows(pos.at[y, c], p_s, p_r, pc_s, pc_r)
-    wo_copy(2, 0).start()
-    for d in (1, 3, 2):
-        wo_copy(d, 1).start()
+    fetches[6].wait()
+    for d in (1, 3, 2):
+        wz_copy(d).start()
+    fetches[0].wait()
+    wo_copy(1).start()
+    wo_copy(3).start()
+    for d in (1, 3, 2):
+        there = turn(z, 4 - d)
+        remote(zgains.at[there], zgains.at[there], f_s.at[d], f_r.at[d], mate).wait_recv()
+        remote(own.at[there], own.at[there], o_s.at[d], o_r.at[d], mate).wait_recv()
+    send_stats(2, *sums_of(own))
     w_step(0)
     w_step(1)
+    input_norm(2, own, a2, lambda g: zgains[g, 1:2, :])
+    spread_rows(a2.at[y, c], by_s, by_r, bc_s, bc_r)
 
     def way_of(s):
         return s // 2
 
-    def ahead(way):
-        return turn(z, 1 + 2 * way)
-
-    def behind(way):
-        return turn(z, 3 - 2 * way)
+    def ahead(way, last):
+        return turn(x if last else z, 1 + 2 * way)
+
+    def owner_at(i, last):
+        return device(i, y, z, c) if last else device(x, y, i, c)
 
     def piece(s):
         return pl.ds(aligned(s * 64, 64), 64)
 
-    def hop_copy(j, s):
-        way = way_of(s)
+    def hop_copy(j, s, last=False):
         return remote(
-            cs.at[j, turn(z, 2), piece(s), :],
+            cs.at[j, turn(x if last else z, 2), piece(s), :],
             hop.at[j, piece(s), :],
             h_s.at[j, s],
             h_r.at[j, s],
-            device(x, y, ahead(way), c),
+            owner_at(ahead(way_of(s), last), last),
         )
 
-    def c_copy(j, s, way):
-        there = ahead(way)
+    def c_copy(j, s, way, last=False):
+        there = ahead(way, last)
         return remote(
             cs.at[j, there, piece(s), :],
             cr.at[way, j, piece(s), :],
             c_s.at[way, j],
             c_r.at[way, j],
-            device(x, y, there, c),
+            owner_at(there, last),
         )
 
-    def c_all(j, way):
+    def c_all(j, way, last=False):
         return remote(
-            cs.at[j, ahead(way)], cr.at[way, j], c_s.at[way, j], c_r.at[way, j], mate
+            cs.at[j, ahead(way, last)], cr.at[way, j], c_s.at[way, j], c_r.at[way, j], mate
         )
 
-    def combine(j, i):
+    def project(j, s, rows, weight, last=False):
+        product = jnp.dot(rows.reshape(256, 1536), weight, preferred_element_type=f32).astype(bf16)
+        for core in range(2):
+            for image in range(4):
+                first = core * 128 + image * 32
+                there = pl.ds(aligned(s * 64 + core * 32, 32), 32)
+                cs[j, image, there, :] = product[first : first + 32]
+        hop_copy(j, s, last).start()
+        c_copy(j, s, 1 - way_of(s), last).start()
+
+    def combine(j, i, last=False):
         s = turn(y, 4 - near(i))
         way = way_of(s)
-        hop_copy(j, s).wait_recv()
-        both = cs[j, ahead(way), piece(s), :].astype(f32) + hop[j, piece(s), :].astype(f32)
-        cs[j, ahead(way), piece(s), :] = both.astype(bf16)
-        c_copy(j, s, way).start()
+        there = ahead(way, last)
+        hop_copy(j, s, last).wait_recv()
+        both = cs[j, there, piece(s), :].astype(f32) + hop[j, piece(s), :].astype(f32)
+        cs[j, there, piece(s), :] = both.astype(bf16)
+        c_copy(j, s, way, last).start()
 
     def att_send(j, heads):
         block = att.at[x, :, pl.ds(aligned(j * 128, 128), heads * 128)]
         for d in (1, 3, 2):
             remote(block, block, t_s.at[d], t_r.at[d], x_peer(d)).start()
 
-    def attend_head(j):
-        c_all(j, 0).wait_recv()
-        c_all(j, 1).wait_recv()
-        projected = cs[j, z].astype(f32) + cr[0, j].astype(f32) + cr[1, j].astype(f32)
+    def attend_head(j, last=False):
+        c_all(j, 0, last).wait_recv()
+        c_all(j, 1, last).wait_recv()
+        projected = cs[j, x if last else z].astype(f32) + cr[0, j].astype(f32) + cr[1, j].astype(f32)
         queries = norm(projected[:, 0:128], qg_ref[...]).astype(bf16)
         keys = norm(projected[:, 128:256], kg_ref[...]).astype(bf16)
         mixed = attention(queries, keys, projected[:, 256:384].astype(bf16), 128 ** (-0.5))
@@ -394,7 +444,7 @@
 
         attend_head(j - 2)
 
-    @pl.loop(0, HEADS_OWN)
+    @pl.loop(0, HEADS_X)
     def _(j):
         @pl.when(j > 2)
         def _():
@@ -419,14 +469,7 @@
                 other = a.at[s, 1 - c]
                 remote(other, other, ac_s.at[e], ac_r.at[e], mate).wait_recv()
 
-            product = jnp.dot(a[s].reshape(256, 1536), w[j], preferred_element_type=f32).astype(bf16)
-            for core in range(2):
-                for image in range(4):
-                    first = core * 128 + image * 32
-                    rows = pl.ds(aligned(s * 64 + core * 32, 32), 32)
-                    cs[j, image, rows, :] = product[first : first + 32]
-            hop_copy(j, s).start()
-            c_copy(j, s, 1 - way_of(s)).start()
+            project(j, s, a[s], w[j])
 
             @pl.when((j == 0) & (i > 0))
             def _():
@@ -447,7 +490,7 @@
         def _():
             earlier_heads(j)
 
-        @pl.when(j + 2 < HEADS_OWN)
+        @pl.when(j + 2 < HEADS_X)
         def _():
             w_step(j + 2)
 
@@ -466,40 +509,52 @@
                 got = pos.at[turn(y, 4 - e), 1 - c]
                 remote(got, got, pc_s.at[e], pc_r.at[e], mate).wait_recv()
 
-        @pl.when((j == 3) | (j == 4))
+        @pl.when(j == 3)
         def _():
             @pl.loop(0, 2)
             def _(i):
-                hidden_heads((j - 3) * 2 + i)
-
-    @pl.loop(0, 2)
-    def _(i):
-        hidden_mix(i)
+                hidden_heads(i)
+
+    for e in (1, 3, 2):
+        got = a2.at[turn(y, 4 - e), c]
+        remote(got, got, by_s.at[e], by_r.at[e], mate).wait_recv()
+        remote(got, got, bc_s.at[e], bc_r.at[e], mate).start()
+    for d in (1, 3, 2):
+        wz_got(d).wait_recv()
 
     @pl.loop(0, 4)
     def _(i):
-        combine(HEADS_OWN - 1, i)
-
-    attend_head(HEADS_OWN - 2)
-    att_send(HEADS_OWN - 2, 1)
+        s = turn(y, 4 - near(i))
+        other = a2.at[s, 1 - c]
+        remote(other, other, bc_s.at[near(i)], bc_r.at[near(i)], mate).wait_recv()
+        project(HEADS_X, s, a2[s], wz[...], True)
+
+    @pl.loop(0, 4)
+    def _(i):
+        combine(HEADS_X - 1, i)
+
+    attend_head(HEADS_X - 2)
+    att_send(HEADS_X - 2, 1)
+
+    @pl.loop(0, 4)
+    def _(i):
+        combine(HEADS_X, i, True)
+
+    wo_copy(2).start()
     fetches[1].wait()
     for d in (1, 3, 2):
-        fgain_copy(d).start()
-        own_copy(d).start()
         ex_copy(d).start()
 
     @pl.loop(2, 4)
     def _(i):
-        hidden_mix(i)
-
-    visible_base()
-    attend_head(HEADS_OWN - 1)
-    att_send(HEADS_OWN - 1, 1)
-    for d in (1, 3, 2):
-        there = turn(z, 4 - d)
-        for half in range(2):
-            block = wo.at[there, 384 * half : 384 * half + 384]
-            remote(block, block, wo_s.at[half, d], wo_r.at[half, d], mate).wait_recv()
+        hidden_heads(i)
+
+    attend_head(HEADS_X - 1)
+    att_send(HEADS_X - 1, 1)
+    attend_head(HEADS_X, True)
+    att_send(HEADS_X, 1)
+    wo_got(1).wait_recv()
+    wo_got(3).wait_recv()
     for d in (1, 3, 2):
         whole = att.at[turn(x, 4 - d)]
         remote(whole, whole, t_s.at[d], t_r.at[d], mate).wait_recv()
@@ -564,6 +619,10 @@
     @pl.loop(0, 4)
     def _(i):
         there = block_at(i)
+
+        @pl.when(i == 3)
+        def _():
+            wo_got(2).wait_recv()
 
         product = jnp.dot(
             att[...].reshape(1024, 768), wo[there], preferred_element_type=f32
@@ -592,10 +651,10 @@
     def enc_copy(d):
         return remote(es.at[turn(z, d)], enc_ref.at[:, z], en_s.at[d], en_r.at[d], z_peer(d))
 
-    for d in (1, 3, 2):
-        there = turn(z, 4 - d)
-        remote(fgains.at[there], fgains.at[there], f_s.at[d], f_r.at[d], mate).wait_recv()
-        remote(own.at[there], own.at[there], o_s.at[d], o_r.at[d], mate).wait_recv()
+    @pl.loop(0, 2)
+    def _(i):
+        hidden_mix(i)
+
     total, square = 0.0, 0.0
     for i in range(4):
         there = block_at(i)
@@ -610,9 +669,11 @@
     for d in (1, 3, 2):
         ex_got(d).wait_recv()
         ec_copy(d).start()
-    average, rate = share_stats(1, total, square)
+    send_stats(1, total, square)
+    visible_base()
+    average, rate = take_stats(1)
     for g in range(4):
-        block = (res[g] - average) * rate * fgains[g, 0:1, :]
+        block = (res[g] - average) * rate * zgains[g, 0:1, :]
         en[:, 384 * g : 384 * g + 384] = block.astype(bf16)
     for d in (1, 3, 2):
         enc_copy(d).start()
@@ -628,6 +689,7 @@
 
     for d in (1, 3, 2):
         eb_copy(d).start()
+    hidden_mix(2)
     embedded = eo[x].astype(f32)
     for d in (1, 3, 2):
         eb_copy(d).wait_recv()
@@ -635,6 +697,7 @@
     vis[row] = (embedded + eb_ref[...]).astype(bf16)
 
     spread_rows(vis.at[row], v_s, v_r, vc_s, vc_r)
+    hidden_mix(3)
 
     for e in (1, 3, 2):
         got = vis.at[turn(y, 4 - e) * 2 + c]
@@ -713,9 +776,10 @@
         gain_copy(d).wait_send()
         raw_copy(d).wait_send()
         own_copy(d).wait_send()
-        fgain_copy(d).wait_send()
-        wo_copy(d, 0).wait_send()
-        wo_copy(d, 1).wait_send()
+        zgain_copy(d).wait_send()
+        wo_copy(d).wait_send()
+        wz_copy(d).wait_send()
+        stat_copy(2, d, x).wait_send()
         stat_copy(0, d, z).wait_send()
         stat_copy(1, d, x).wait_send()
         ex_copy(d).wait_send()
@@ -726,6 +790,7 @@
     for e in range(4):
         for block, s_y, r_y, s_c, r_c in (
             (a, ay_s, ay_r, ac_s, ac_r),
+            (a2, by_s, by_r, bc_s, bc_r),
             (pos, p_s, p_r, pc_s, pc_r),
         ):
             if e > 0:
@@ -745,7 +810,7 @@
     for k in range(1, 8):
         mix_copy(k // 2, k % 2).wait_send()
 
-    @pl.loop(0, HEADS_OWN)
+    @pl.loop(0, HEADS_X)
     def _(j):
         for way in range(2):
             w_send(j, way).wait_send()
@@ -815,9 +880,11 @@
             pltpu.VMEM((4, 8, 384), f32),
             pltpu.VMEM((4, 4, 32, 384), bf16),
             pltpu.VMEM((4, 4, 32, 384), bf16),
-            pltpu.VMEM((2, 4, 8, 128), f32),
+            pltpu.VMEM((3, 4, 8, 128), f32),
             pltpu.VMEM((4, 2, 128, 1536), bf16),
-            pltpu.VMEM((HEADS_OWN, 1536, 384), bf16),
+            pltpu.VMEM((4, 2, 128, 1536), bf16),
+            pltpu.VMEM((HEADS_X, 1536, 384), bf16),
+            pltpu.VMEM((1536, 384), bf16),
             pltpu.VMEM((4, 768, 384), bf16),
             pltpu.VMEM((HEADS_OWN, 4, 256, 384), bf16),
             pltpu.VMEM((2, HEADS_OWN, 256, 384), bf16),
@@ -851,18 +918,21 @@
             pltpu.VMEM((256, 256), bf16),
             pltpu.VMEM((8, 128, 128), bf16),
             pltpu.VMEM((128, DD), bf16),
-            dma((6,)),
-            dma((HEADS_OWN,)),
-            *two,
-            *two,
-            *two,
-            *two,
-            dma((2, 4)), dma((2, 4)),
-            dma((2, 4)), dma((2, 4)),
-            *two,
-            *two,
-            dma((2, HEADS_OWN)), dma((2, HEADS_OWN)),
-            dma((2, HEADS_OWN)), dma((2, HEADS_OWN)),
+            dma((7,)),
+            dma((HEADS_X,)),
+            *two,
+            *two,
+            *two,
+            *two,
+            *two,
+            *two,
+            dma((3, 4)), dma((3, 4)),
+            *two,
+            *two,
+            *two,
+            *two,
+            dma((2, HEADS_X)), dma((2, HEADS_X)),
+            dma((2, HEADS_X)), dma((2, HEADS_X)),
             dma((HEADS_OWN, 4)), dma((HEADS_OWN, 4)),
             dma((2, HEADS_OWN)), dma((2, HEADS_OWN)),
             *two,

time: 148 us -> 153 us (1.034)
  Pallas kernels: 146 us -> 152 us
    pallas_call x1, Pallas kernels: 144 us -> 150 us  [local(): pl.pallas_call(kernel, out_shape=(jax.ShapeDtypeStruct((4, 4, 32, 384), b...]
where the time goes in v8:
time: 153 us
  Pallas kernels  152 us (99%)
    pallas_call x1, Pallas kernels, local(): pl.pallas_call(kernel, out_shape=(jax.ShapeDtypeStruct((4, 4, 32, 384), b...  150 us

profile of v8, /device:TPU:1, one launch (start us, length us, event | category | flops | bytes accessed | tf_op | source)
XLA Modules:
  0.0 153.1 jit_solution(1298906103750108532)
XLA Ops:
  1.3 149.9 %masked_patches.1 = (bf16[4,4,32,384]{3,2,1,0:T(8,128)(2,1)}, bf16[1,128,768]{2,1,0:T(8,128)(2,1)}) custom-call(bf16[4,4,32,384]{3,2,1,0:T(8,128)(2,1)} %bitcast.12, f32[384]{0:T(512)} %ig_ref.1, bf16[384,2304]{1,0:T(8,128)(2,1)} %w_ref.1, f32[1,128]{1,0:T(1,128)} %bitcast.18, f32[1,128]{1,0:T(1,128)} %bitcast.19, bf16[768,384]{1,0:T(8,128)(2,1)} %wo_ref.1, ...), custom_call_target="tpu_custom_call" | custom-call | tf_op jit(solution)/shard_map/masked_patches/pallas_call | solution.py:867
  151.2 1.9 %hand_on.1 = (bf16[16,32,384]{2,1,0:T(8,128)(2,1)}, bf16[1,128,768]{2,1,0:T(8,128)(2,1)}) custom-call(bf16[16,32,384]{2,1,0:T(8,128)(2,1)} %bitcast.13, bf16[1,128,768]{2,1,0:T(8,128)(2,1)} %get-tuple-element.5.pred_ref), custom_call_target="tpu_custom_call" | custom-call | tf_op jit(solution)/shard_map/hand_on/pallas_call | solution.py:964

commit v9 on v7

--- a/solution.py
+++ b/solution.py
@@ -71,12 +71,28 @@
     return (mixture / totals).astype(bf16)
 
 
-def kernel(
+SMALL = (1, 3, 4, 6, 8, 9, 11, 12, 14, 15, 17, 19, 20, 21)
+
+
+def kernel(*refs):
+    operands, outputs, rest = list(refs[:22]), refs[22:24], refs[24:]
+    held, sems, rest = rest[: len(SMALL)], rest[len(SMALL)], rest[len(SMALL) + 1 :]
+    small = []
+    for k, index in enumerate(SMALL):
+        small.append(pltpu.make_async_copy(operands[index], held[k], sems.at[k]))
+        operands[index] = held[k]
+    for copy in small:
+        copy.start()
+    body(small, *operands, *outputs, *rest)
+
+
+def body(
+    small,
     x_ref, ig_ref, w_ref, qg_ref, kg_ref, wo_ref, fg_ref, ew_ref, eb_ref, mask_ref, pos_ref,
     script_ref, dg_ref, dp_ref, dqg_ref, dkg_ref, do_ref, hg_ref, pw_ref, pb_ref, vi_ref, si_ref,
     enc_ref, pred_ref,
     gains, fgains, raw, own, stats, a, w, wo, cs, cr, hop, att, po, pr, yr, yhop, res, en, es, ew, pos, dpw, dow, pxw,
-    eo, er, vis, scr, sel, tok, tokv, dq, dk, dv, base, vq, vk, vv, dm, da,
+    eo, er, vis, scr, sel, tok, tokv, dq, dk, dv, base, vq, vk, vv, dm, da, pred,
     l_s, w_s, g_s, g_r, f_s, f_r, x_s, x_r, o_s, o_r, wo_s, wo_r, st_s, st_r, ay_s, ay_r, ac_s, ac_r, wn_s, wn_r, wf_s, wf_r,
     h_s, h_r, c_s, c_r, t_s, t_r, p_s, p_r, pc_s, pc_r, ex_s, ex_r, ec_s, ec_r,
     m_s, m_r, yh_s, yh_r, y_s, y_r, en_s, en_r, eb_s, eb_r, v_s, v_r, vc_s, vc_r, d_s, d_r,
@@ -124,9 +140,6 @@
         pltpu.make_async_copy(pw_ref, pxw, l_s.at[5]),
     ]
 
-    gains[x] = jnp.broadcast_to(ig_ref[...].reshape(1, 384), (8, 384))
-    fgains[z] = jnp.broadcast_to(fg_ref[...].reshape(1, 384), (8, 384))
-
     barrier = pltpu.get_barrier_semaphore()
     peers = (
         [x_peer(d) for d in range(1, 4)]
@@ -135,6 +148,16 @@
     )
     for peer in peers:
         pl.semaphore_signal(barrier, inc=1, device_id=peer, device_id_type=MESH)
+    mine = [
+        pltpu.make_async_copy(x_ref.at[x], raw.at[x], l_s.at[6]),
+        pltpu.make_async_copy(x_ref.at[:, z], own.at[z], l_s.at[7]),
+    ]
+    for copy in mine:
+        copy.start()
+    for copy in small:
+        copy.wait()
+    gains[x] = jnp.broadcast_to(ig_ref[...].reshape(1, 384), (8, 384))
+    fgains[z] = jnp.broadcast_to(fg_ref[...].reshape(1, 384), (8, 384))
     pl.semaphore_wait(barrier, len(peers))
 
     def raw_copy(d):
@@ -158,8 +181,6 @@
         raw_copy(d).start()
     for fetch in fetches:
         fetch.start()
-    raw[x] = x_ref[x]
-    own[z] = x_ref[:, z]
 
     def w_send(j, way):
         block = w_block(j, x, 0, 384)
@@ -219,6 +240,8 @@
         spread = sums[:, 1:2] / D - average * average
         return average, lax.rsqrt(spread + epsilon)
 
+    for copy in mine:
+        copy.wait()
     for d in (1, 3, 2):
         there = turn(x, 4 - d)
         remote(gains.at[there], gains.at[there], g_s.at[d], g_r.at[d], mate).wait_recv()
@@ -403,6 +426,10 @@
         w_far(j, 0).wait_recv()
         w_far(j, 1).wait_recv()
 
+        @pl.when(j + 2 < HEADS_OWN)
+        def _():
+            w_step(j + 2)
+
         @pl.loop(0, 4)
         def _(i):
             e = near(i)
@@ -446,10 +473,6 @@
         @pl.when(j == 2)
         def _():
             earlier_heads(j)
-
-        @pl.when(j + 2 < HEADS_OWN)
-        def _():
-            w_step(j + 2)
 
         @pl.when(j == 3)
         def _():
@@ -616,7 +639,8 @@
         en[:, 384 * g : 384 * g + 384] = block.astype(bf16)
     for d in (1, 3, 2):
         enc_copy(d).start()
-    enc_ref[:, z] = es[z]
+    enc_mine = pltpu.make_async_copy(es.at[z], enc_ref.at[:, z], l_s.at[8])
+    enc_mine.start()
 
     for d in (1, 3, 2):
         ec_got(d).wait_recv()
@@ -704,8 +728,11 @@
     decoded = tokens + jnp.dot(da[...], dow[...], preferred_element_type=f32)
     normed = norm(decoded, hg_ref[...]).astype(bf16)
     predicted = jnp.dot(normed, pxw[...], preferred_element_type=f32) + pb_ref[...].reshape(1, 768)
-    pred_ref[0] = predicted.astype(bf16)
-
+    pred[...] = predicted.astype(bf16)
+    pred_mine = pltpu.make_async_copy(pred, pred_ref.at[0], l_s.at[9])
+    pred_mine.start()
+
+    enc_mine.wait()
     for d in range(1, 4):
         block = enc_ref.at[:, turn(z, 4 - d)]
         remote(block, block, en_s.at[d], en_r.at[d], mate).wait_recv()
@@ -759,6 +786,7 @@
         @pl.loop(0, 4)
         def _(s):
             hop_copy(j, s).wait_send()
+    pred_mine.wait()
 
 
 def hand_on(enc_ref, pred_ref, enc_out, pred_out):
@@ -799,18 +827,24 @@
 
     dma = pltpu.SemaphoreType.DMA
     two = [dma((4,)), dma((4,))]
+    operands = (
+        visible_patches.reshape(4, 4, 32, 384), input_gain, encoder_project, flat(query_gain), flat(key_gain),
+        output_weight, final_gain, embed_weight, flat(embed_bias), flat(mask_token),
+        position_embed, script_table, flat(decoder_gain), decoder_project, flat(decoder_query),
+        flat(decoder_key), decoder_output, flat(head_gain), pixel_weight, pixel_bias,
+        visible_index, flat(script_index),
+    )
     encoded, predicted = pl.pallas_call(
         kernel,
         out_shape=(
             jax.ShapeDtypeStruct((4, 4, 32, 384), bf16),
             jax.ShapeDtypeStruct((1, 128, 768), bf16),
         ),
-        in_specs=[
-            VMEM, VMEM, ANY, VMEM, VMEM, ANY, VMEM, ANY, VMEM, VMEM, ANY,
-            VMEM, VMEM, ANY, VMEM, VMEM, ANY, VMEM, ANY, VMEM, VMEM, VMEM,
-        ],
-        out_specs=(VMEM, VMEM),
+        in_specs=[ANY] * 22,
+        out_specs=(ANY, ANY),
         scratch_shapes=[
+            *[pltpu.VMEM(operands[index].shape, operands[index].dtype) for index in SMALL],
+            dma((len(SMALL),)),
             pltpu.VMEM((4, 8, 384), f32),
             pltpu.VMEM((4, 8, 384), f32),
             pltpu.VMEM((4, 4, 32, 384), bf16),
@@ -851,7 +885,8 @@
             pltpu.VMEM((256, 256), bf16),
             pltpu.VMEM((8, 128, 128), bf16),
             pltpu.VMEM((128, DD), bf16),
-            dma((6,)),
+            pltpu.VMEM((128, 768), bf16),
+            dma((10,)),
             dma((HEADS_OWN,)),
             *two,
             *two,
@@ -883,13 +918,7 @@
             collective_id=0, has_side_effects=True, vmem_limit_bytes=62 << 20
         ),
         name="masked_patches",
-    )(
-        visible_patches.reshape(4, 4, 32, 384), input_gain, encoder_project, flat(query_gain), flat(key_gain),
-        output_weight, final_gain, embed_weight, flat(embed_bias), flat(mask_token),
-        position_embed, script_table, flat(decoder_gain), decoder_project, flat(decoder_query),
-        flat(decoder_key), decoder_output, flat(head_gain), pixel_weight, pixel_bias,
-        visible_index, flat(script_index),
-    )
+    )(*operands)
     encoded = encoded.reshape(16, 32, 384)
     return pl.pallas_call(
         hand_on,

time: 148 us -> 147 us (level)
  no operation moved by 1% of the time
where the time goes in v9:
time: 147 us; the launch traced here: 146 us
  Pallas kernels  145 us (99%)
    pallas_call x1, Pallas kernels, local(): pl.pallas_call(kernel, out_shape=(jax.ShapeDtypeStruct((4, 4, 32, 384), b...  143 us

profile of v9, /device:TPU:1, one launch (start us, length us, event | category | flops | bytes accessed | tf_op | source)
XLA Modules:
  0.0 146.4 jit_solution(18059201567103316609)
XLA Ops:
  1.3 143.2 %masked_patches.1 = (bf16[4,4,32,384]{3,2,1,0:T(8,128)(2,1)}, bf16[1,128,768]{2,1,0:T(8,128)(2,1)}) custom-call(bf16[4,4,32,384]{3,2,1,0:T(8,128)(2,1)} %bitcast.12, f32[384]{0:T(512)} %refs_1_.1, bf16[384,2304]{1,0:T(8,128)(2,1)} %refs_2_.1, f32[1,128]{1,0:T(1,128)} %bitcast.18, f32[1,128]{1,0:T(1,128)} %bitcast.19, bf16[768,384]{1,0:T(8,128)(2,1)} %refs_5_.1, ...), custom_call_target="tpu_custom_call" | custom-call | tf_op jit(solution)/shard_map/masked_patches/pallas_call | solution.py:837
  144.5 1.9 %hand_on.1 = (bf16[16,32,384]{2,1,0:T(8,128)(2,1)}, bf16[1,128,768]{2,1,0:T(8,128)(2,1)}) custom-call(bf16[16,32,384]{2,1,0:T(8,128)(2,1)} %bitcast.13, bf16[1,128,768]{2,1,0:T(8,128)(2,1)} %get-tuple-element.5.pred_ref), custom_call_target="tpu_custom_call" | custom-call | tf_op jit(solution)/shard_map/hand_on/pallas_call | solution.py:923

commit v10 on v9

--- a/solution.py
+++ b/solution.py
@@ -211,13 +211,12 @@
         w_got(j, 1).wait_recv()
         w_forward(j, 1).start()
 
-        @pl.when(j + 3 < HEADS_OWN)
-        def _():
-            w_start(j + 3)
+        @pl.when(j + 2 < HEADS_OWN)
+        def _():
+            w_start(j + 2)
 
     w_start(0)
     w_start(1)
-    w_start(2)
     fetches[0].wait()
     wo_copy(1, 0).start()
     wo_copy(3, 0).start()

time: 147 us -> 147 us (level)
  no operation moved by 1% of the time
where the time goes in v10:
time: 147 us; the launch traced here: 146 us
  Pallas kernels  145 us (99%)
    pallas_call x1, Pallas kernels, local(): pl.pallas_call(kernel, out_shape=(jax.ShapeDtypeStruct((4, 4, 32, 384), b...  143 us

profile of v10, /device:TPU:1, one launch (start us, length us, event | category | flops | bytes accessed | tf_op | source)
XLA Modules:
  0.0 146.4 jit_solution(1488052190060388136)
XLA Ops:
  1.3 143.2 %masked_patches.1 = (bf16[4,4,32,384]{3,2,1,0:T(8,128)(2,1)}, bf16[1,128,768]{2,1,0:T(8,128)(2,1)}) custom-call(bf16[4,4,32,384]{3,2,1,0:T(8,128)(2,1)} %bitcast.12, f32[384]{0:T(512)} %refs_1_.1, bf16[384,2304]{1,0:T(8,128)(2,1)} %refs_2_.1, f32[1,128]{1,0:T(1,128)} %bitcast.18, f32[1,128]{1,0:T(1,128)} %bitcast.19, bf16[768,384]{1,0:T(8,128)(2,1)} %refs_5_.1, ...), custom_call_target="tpu_custom_call" | custom-call | tf_op jit(solution)/shard_map/masked_patches/pallas_call | solution.py:836
  144.5 1.9 %hand_on.1 = (bf16[16,32,384]{2,1,0:T(8,128)(2,1)}, bf16[1,128,768]{2,1,0:T(8,128)(2,1)}) custom-call(bf16[16,32,384]{2,1,0:T(8,128)(2,1)} %bitcast.13, bf16[1,128,768]{2,1,0:T(8,128)(2,1)} %get-tuple-element.5.pred_ref), custom_call_target="tpu_custom_call" | custom-call | tf_op jit(solution)/shard_map/hand_on/pallas_call | solution.py:922
